TPU v7x, 512 devices: a whole 4x4x16 slice. The times are simulated.
512 devices in a mesh: dp: 4 (over z_hi), seq: 32 (over y, z_lo, core), tile: 4 (over x).
Axes of the slice: x: 4, y: 4, z: 16 (z_hi: 4, z_lo: 4; z = z_hi * 4 + z_lo), core: 2. Of those that a mesh axis runs over, the one named last changes fastest.
Arguments:
- latents: bfloat16 [4, 32, 512, 1152], P('dp', 'seq', 'tile'), may hold values from -6 to 6
- upstream: bfloat16 [4, 32, 512, 1152], P('dp', 'seq', 'tile'), may hold values from -6 to 6
- modulation: float32 [4, 2, 1152], P('dp'), may hold values from -0.5 to 6
- space_qkv: bfloat16 [1152, 1728], P(('dp', 'tile')), may hold values from -1 to 1
- space_out: bfloat16 [576, 1152], P(('dp', 'tile')), may hold values from -0.25 to 0.25
- time_qkv: bfloat16 [1152, 1728], P(('dp', 'tile')), may hold values from -1 to 1
- time_out: bfloat16 [576, 1152], P(('dp', 'tile')), may hold values from -0.25 to 0.25
- space_pattern: int32 [8, 4], P('tile'), may hold values 0 or 1
- time_mask: int32 [32, 32], replicated, may hold values 0 or 1
Outputs:
- result: bfloat16 [4, 32, 512, 1152], P('dp', 'seq', 'tile')
- start_grad: bfloat16 [4, 32, 512, 1152], P('dp', 'seq', 'tile')
- time_out_grad: float32 [576, 1152], P(('dp', 'tile'))
All inputs are finite; a program needn't handle non-finite values. No bound on the sum of `space_pattern` on one device may be relied on, other than what follows from the above.
Results may differ from a plain program's by a relative error of at most 0.035.
Values may be sent and summed in bfloat16 or wider, within the bound.
A program may use at most 64 MiB of HBM per device.

v0:
```python
import jax
import jax.numpy as jnp
from jax import lax
from jax.sharding import PartitionSpec as P

HEADS = 8
HEAD_DIM = 72


EPSILON = 1e-06
MASKED = -1e30


def extended(block, sides, width):
    for axis, dim in sides:
        count = lax.axis_size(axis)
        forward = [(i, i + 1) for i in range(count - 1)]
        backward = [(target, source) for source, target in forward]
        low = lax.ppermute(
            lax.slice_in_dim(block, block.shape[dim] - width, None, axis=dim), axis, forward
        )
        high = lax.ppermute(lax.slice_in_dim(block, 0, width, axis=dim), axis, backward)
        block = jnp.concatenate([low, block, high], axis=dim)
    return block


def shifted(array, axis, by):
    devices = lax.axis_size(axis)
    pairs = [(i, i + by) for i in range(devices) if 0 <= i + by < devices]
    return lax.ppermute(array, axis, pairs)


def heads(rows):
    return rows.reshape(rows.shape[:-1] + (HEADS, HEAD_DIM))


def merged(rows):
    return rows.reshape(rows.shape[:-2] + (HEADS * HEAD_DIM,))


def split(rows):
    width = HEADS * HEAD_DIM
    return (
        heads(rows[..., :width]),
        heads(rows[..., width : 2 * width]),
        heads(rows[..., 2 * width :]),
    )


def project(rows, weight):
    flat = rows.reshape(-1, rows.shape[-1])
    out = jnp.dot(flat, weight, preferred_element_type=jnp.float32)
    return out.reshape(rows.shape[:-1] + (weight.shape[1],))


def project_back(rows, weight):
    flat = rows.reshape(-1, rows.shape[-1])
    out = jnp.einsum("rk,dk->rd", flat, weight, preferred_element_type=jnp.float32)
    return out.reshape(rows.shape[:-1] + (weight.shape[0],))


def norm_scale(values, gain):
    inverse = lax.rsqrt(jnp.mean(values * values, axis=-1, keepdims=True) + EPSILON)
    return (inverse, values * inverse * gain)


def norm_back(values, inverse, gain, grad):
    scaled = grad * gain
    cubed = inverse * inverse * inverse
    return inverse * scaled - values * cubed * jnp.mean(scaled * values, axis=-1, keepdims=True)


def forms(lead):
    if lead:
        return ("cbqhe", "cbkhe")
    return ("cqbhe", "ckbhe")


def weights_of(query, keys, allowed, lead):
    qform, kform = forms(lead)
    scores = jnp.einsum(
        qform + "," + kform + "->cbhqk", query, keys, preferred_element_type=jnp.float32
    )
    scores = jnp.where(allowed, scores * HEAD_DIM ** (-0.5), MASKED)
    top = jnp.max(scores, axis=-1, keepdims=True)
    raised = jnp.exp(scores - top)
    return raised / jnp.sum(raised, axis=-1, keepdims=True)


def attend(query, keys, values, allowed, lead):
    qform, kform = forms(lead)
    probs = weights_of(query, keys, allowed, lead)
    out = jnp.einsum(
        "cbhqk," + kform + "->" + qform,
        probs.astype(jnp.bfloat16),
        values,
        preferred_element_type=jnp.float32,
    )
    return (out.astype(jnp.bfloat16), probs)


def attend_back(query, keys, values, probs, grad_out, lead):
    qform, kform = forms(lead)
    dprob = jnp.einsum(
        qform + "," + kform + "->cbhqk", grad_out, values, preferred_element_type=jnp.float32
    )
    delta = jnp.sum(probs * dprob, axis=-1, keepdims=True)
    dscore = (probs * (dprob - delta) * HEAD_DIM ** (-0.5)).astype(jnp.bfloat16)
    dquery = jnp.einsum(
        "cbhqk," + kform + "->" + qform, dscore, keys, preferred_element_type=jnp.float32
    )
    dkeys = jnp.einsum(
        "cbhqk," + qform + "->" + kform, dscore, query, preferred_element_type=jnp.float32
    )
    dvalues = jnp.einsum(
        "cbhqk," + qform + "->" + kform,
        probs.astype(jnp.bfloat16),
        grad_out,
        preferred_element_type=jnp.float32,
    )
    return (dquery, dkeys, dvalues)


def time_ok(time_mask):
    frame = jnp.arange(time_mask.shape[0])
    return (frame[None, :] == frame[:, None]) | (frame[None, :] < frame[:, None]) & (time_mask == 1)


def local(
    latents,
    upstream,
    modulation,
    space_qkv,
    space_out,
    time_qkv,
    time_out,
    space_pattern,
    time_mask,
):
    width = HEADS * HEAD_DIM
    own = latents.shape[2]
    span = own // 2
    space_qkv_all, space_out_all = (
        lax.all_gather(space_qkv, ("dp", "tile"), axis=0, tiled=True),
        lax.all_gather(space_out, ("dp", "tile"), axis=0, tiled=True),
    )
    start = latents.astype(jnp.float32)
    gain_space = 1.0 + modulation[:, 0][:, None, None, :]
    gain_time = 1.0 + modulation[:, 1][:, None, None, :]
    inverse_space, normed = norm_scale(start, gain_space)
    space_rows = project(normed.astype(jnp.bfloat16), space_qkv_all).astype(jnp.bfloat16)
    query = heads(space_rows[..., :width])
    window = extended(space_rows[..., width:], (("tile", 2),), span)
    keys = heads(window[..., :width])
    values = heads(window[..., width:])
    tile_at = lax.axis_index("tile")
    tiles = lax.axis_size("tile")
    slots = jnp.arange(4)
    block_ok = (space_pattern == 1) | (slots[None, :] == jnp.arange(2)[:, None] + 1)
    global_block = 2 * tile_at - 1 + slots
    block_ok = block_ok & ((global_block >= 0) & (global_block < 2 * tiles))[None, :]
    allowed = jnp.repeat(jnp.repeat(block_ok, span, axis=0), span, axis=1)[None, None, None]
    space_heads, space_probs = attend(query, keys, values, allowed, True)
    space_att = merged(space_heads)
    middle = start + project(space_att, space_out_all)
    time_qkv_all, time_out_all = (
        lax.all_gather(time_qkv, ("dp", "tile"), axis=0, tiled=True),
        lax.all_gather(time_out, ("dp", "tile"), axis=0, tiled=True),
    )
    inverse_time, normed_time = norm_scale(middle, gain_time)
    normed_time = normed_time.astype(jnp.bfloat16)
    frame_mask = time_ok(time_mask)[None, None, None]
    time_local = project(normed_time, time_qkv_all).astype(jnp.bfloat16)
    rows = lax.all_to_all(time_local, "seq", split_axis=2, concat_axis=1, tiled=True)
    time_query, time_keys, time_values = split(rows)
    out, probs = attend(time_query, time_keys, time_values, frame_mask, False)
    time_patches = merged(out)
    time_att = lax.all_to_all(time_patches, "seq", split_axis=1, concat_axis=2, tiled=True)
    result = (middle + project(time_att, time_out_all)).astype(jnp.bfloat16)
    flat_up = upstream.reshape(-1, upstream.shape[-1])
    term = jnp.einsum(
        "rh,rd->hd", time_att.reshape(-1, width), flat_up, preferred_element_type=jnp.float32
    )
    rows_part = lax.psum_scatter(
        term.astype(jnp.bfloat16), ("dp", "tile"), scatter_dimension=0, tiled=True
    )
    time_out_grad = lax.psum(rows_part, "seq").astype(jnp.float32)
    grad_att = project_back(upstream, time_out_all).astype(jnp.bfloat16)
    grad_patches = lax.all_to_all(grad_att, "seq", split_axis=2, concat_axis=1, tiled=True)
    time_query, time_keys, time_values = split(rows)
    time_probs = weights_of(time_query, time_keys, frame_mask, False)
    gq, gk, gv = attend_back(
        time_query, time_keys, time_values, time_probs, heads(grad_patches), False
    )
    patch_grads = jnp.concatenate([merged(gq), merged(gk), merged(gv)], axis=-1).astype(
        jnp.bfloat16
    )
    time_grads = lax.all_to_all(patch_grads, "seq", split_axis=1, concat_axis=2, tiled=True)
    middle_grad = upstream.astype(jnp.float32) + norm_back(
        middle, inverse_time, gain_time, project_back(time_grads, time_qkv_all)
    )
    space_grad_att = project_back(middle_grad.astype(jnp.bfloat16), space_out_all).astype(
        jnp.bfloat16
    )
    dq, dk, dv = attend_back(query, keys, values, space_probs, heads(space_grad_att), True)
    rim = jnp.concatenate([merged(dk), merged(dv)], axis=-1)
    from_right = shifted(rim[:, :, :span].astype(jnp.bfloat16), "tile", -1).astype(jnp.float32)
    from_left = shifted(rim[:, :, span + own :].astype(jnp.bfloat16), "tile", 1).astype(jnp.float32)
    own_grads = rim[:, :, span : span + own] + jnp.concatenate([from_left, from_right], axis=2)
    space_grads = jnp.concatenate([merged(dq), own_grads], axis=-1).astype(jnp.bfloat16)
    start_grad = middle_grad + norm_back(
        start, inverse_space, gain_space, project_back(space_grads, space_qkv_all)
    )
    return (result, start_grad.astype(jnp.bfloat16), time_out_grad)


def solution(mesh):
    in_specs = (
        P("dp", "seq", "tile", None),
        P("dp", "seq", "tile", None),
        P("dp", None, None),
        P(("dp", "tile"), None),
        P(("dp", "tile"), None),
        P(("dp", "tile"), None),
        P(("dp", "tile"), None),
        P("tile", None),
        P(),
    )
    out_specs = (
        P("dp", "seq", "tile", None),
        P("dp", "seq", "tile", None),
        P(("dp", "tile"), None),
    )
    return jax.shard_map(local, mesh=mesh, in_specs=in_specs, out_specs=out_specs, check_vma=False)
```

profile of v0, /device:TPU:1, one launch (start us, length us, event | category | flops | bytes accessed | tf_op | source)
XLA Modules:
  0.0 1007.5 jit_solution(9956901177257667896)
XLA Ops:
  14.2 86.8 %all-gather.13.cloned.1.call-done = bf16[16,36,1152]{2,1,0:T(8,128)(2,1)} async-done(((bf16[1,36,1152]{2,1,0:T(8,128)(2,1)}), bf16[16,36,1152]{2,1,0:T(8,128)(2,1)}) %all-gather.13.cloned.1.call-update) | async-done | bytes 1327120 | tf_op jit(solution)/shard_map/all_gather | solution.py:168
  101.0 2.2 reshape.419
  103.3 129.2 %all-gather.7.cloned.1.call-done = bf16[1152,1728]{1,0:T(8,128)(2,1)} async-done(((bf16[72,1728]{1,0:T(8,128)(2,1)}), bf16[1152,1728]{1,0:T(8,128)(2,1)}) %all-gather.7.cloned.1.call-update) | async-done | bytes 3981328 | tf_op jit(solution)/shard_map/all_gather | solution.py:144
  232.5 3.8 fusion.8
  237.2 4.3 collective-permute-start
  246.7 5.8 all-to-all-start.2
  252.5 64.3 %all-gather.11.cloned.1.call-done = bf16[16,36,1152]{2,1,0:T(8,128)(2,1)} async-done(((bf16[1,36,1152]{2,1,0:T(8,128)(2,1)}), bf16[16,36,1152]{2,1,0:T(8,128)(2,1)}) %all-gather.11.cloned.1.call-update) | async-done | bytes 1327120 | tf_op jit(solution)/shard_map/all_gather | solution.py:145
  316.8 2.2 reshape.417
  322.1 3.3 fusion.105
  325.3 2.4 convolution_convert_fusion.8
  329.8 118.4 %all-gather.9.cloned.1.call-done = bf16[1152,1728]{1,0:T(8,128)(2,1)} async-done(((bf16[72,1728]{1,0:T(8,128)(2,1)}), bf16[1152,1728]{1,0:T(8,128)(2,1)}) %all-gather.9.cloned.1.call-update) | async-done | bytes 3981328 | tf_op jit(solution)/shard_map/all_gather | solution.py:167
  448.1 4.6 fusion.9
  452.7 3.1 copy.67
  455.8 5.2 reduce.24
  461.0 2.3 reshape.429
  463.3 6.0 all-to-all-start
  472.1 2.1 reshape.432
  474.2 2.6 bitcast_reduce_fusion.1
  478.7 5.8 all-to-all-done
  484.5 3.9 reshape.430
  488.5 4.5 bitcast_reduce_fusion
  493.0 1.9 all_to_all.11
  494.9 2.0 fusion.103
  496.9 1.9 reshape.423
  498.8 1.9 reshape.424
  502.7 2.8 fusion.106
  509.6 4.4 all-to-all-start.1
  513.9 2.1 fusion.79
  516.0 2.7 fusion.27
  522.3 2.7 fusion.26
  532.6 2.0 concatenate.45
  534.6 2.2 copy.88
  536.8 7.8 all-to-all-start.3
  546.3 2.7 convolution_convert_fusion
  549.0 87.2 %fusion = bf16[48,1152]{1,0:T(8,128)(2,1)} fusion(bf16[576,1152]{1,0:T(8,128)(2,1)} %convolution_convert_fusion), kind=kCustom, calls=%all-reduce-scatter | all-reduce-scatter fusion | flops 884737 | bytes 1439744
  636.1 1.9 collective-permute-start.6
  638.1 2.2 collective-permute-start.5
  640.3 2.7 collective-permute-start.4
  644.5 1.9 collective-permute-start.7
  648.3 8.0 concatenate.52
  657.9 2.0 fusion.7
  659.9 299.7 %all-reduce.4.cloned.1.call-done = bf16[36,1152]{1,0:T(8,128)(2,1)} async-done(((bf16[36,1152]{1,0:T(8,128)(2,1)}), bf16[36,1152]{1,0:T(8,128)(2,1)}) %all-reduce.4.cloned.1.call-update) | async-done | bytes 82960 | tf_op jit(solution)/shard_map/psum | solution.py:187
  961.2 2.0 reshape.411
  963.2 3.8 fusion.50
  971.1 8.7 fusion.30
  982.0 3.5 collective-permute-start.2
  986.9 7.9 convolution_convert_fusion.7
  996.2 3.7 fusion.46
  (108 shorter events, 57.3 us)
Async XLA Ops:
  7.2 93.9 %all-gather.13.cloned.1.call-start = ((), (), s32[]{:S(2)}) async-start(), calls=%async_computation.8 | async-start | bytes 1566720 | tf_op jit(solution)/shard_map/all_gather | solution.py:168
  7.9 224.6 %all-gather.7.cloned.1.call-start = ((), (), s32[]{:S(2)}) async-start(), calls=%async_computation.4 | async-start | bytes 4386816 | tf_op jit(solution)/shard_map/all_gather | solution.py:144
  8.6 308.2 %all-gather.11.cloned.1.call-start = ((), (), s32[]{:S(2)}) async-start(), calls=%async_computation.7 | async-start | bytes 1566720 | tf_op jit(solution)/shard_map/all_gather | solution.py:145
  9.4 438.7 %all-gather.9.cloned.1.call-start = ((), (), s32[]{:S(2)}) async-start(), calls=%async_computation.5 | async-start | bytes 4386816 | tf_op jit(solution)/shard_map/all_gather | solution.py:167
  14.2 218.2 %copy-start.11 = (f32[128]{0:T(128)}, f32[128]{0:T(128)S(1)}, u32[]{:S(2)}) copy-start(f32[128]{0:T(128)S(1)} %get-tuple-element.15) | copy-start | bytes 1540
  14.2 218.2 %copy-start = (bf16[1,1,128,1152]{3,2,1,0:T(8,128)(2,1)S(1)}, bf16[1,1,128,1152]{3,2,1,0:T(8,128)(2,1)}, u32[]{:S(2)}) copy-start(bf16[1,1,128,1152]{3,2,1,0:T(8,128)(2,1)} %param.9) | copy-start | bytes 884740
  236.3 6.5 copy-start.1
  237.2 82.5 %collective-permute-start = (bf16[1,1,64,1152]{2,3,1,0:T(8,128)(2,1)}, bf16[1,1,64,1152]{2,3,1,0:T(8,128)(2,1)}, u32[]{:S(2)}, u32[]{:S(2)}) collective-permute-start(bf16[1,1,64,1152]{2,3,1,0:T(8,128)(2,1)} %get-tuple-element.12), channel_id=1, source_target_pairs={{0,1},{1,2},{2,3},{4,5},{5,6},{6,7},{8,9},{9,10},{10,11},{12,13},{... | collective-permute-start | bytes 442376 | tf_op jit(solution)/shard_map/ppermute | solution.py:19
  241.6 78.2 %collective-permute-start.1 = (bf16[1,1,64,1152]{2,3,1,0:T(8,128)(2,1)}, bf16[1,1,64,1152]{2,3,1,0:T(8,128)(2,1)}, u32[]{:S(2)}, u32[]{:S(2)}) collective-permute-start(bf16[1,1,64,1152]{2,3,1,0:T(8,128)(2,1)} %get-tuple-element.13), channel_id=1, source_target_pairs={{1,0},{2,1},{3,2},{5,4},{6,5},{7,6},{9,8},{10,9},{11,10},{13,12},{... | collective-permute-start | bytes 442376 | tf_op jit(solution)/shard_map/ppermute | solution.py:22
  246.7 216.7 %all-to-all-start.2 = ((bf16[32,2,1152]{2,1,0:T(2,128)(2,1)}), bf16[32,2,1152]{2,1,0:T(2,128)(2,1)}, u32[]{:S(2)}, u32[]{:S(2)}) async-start(bf16[32,2,1152]{2,1,0:T(2,128)(2,1)} %reshape.431), calls=%async_computation.2 | async-start | bytes 294912 | tf_op jit(solution)/shard_map/all_to_all | solution.py:189
  322.1 3.3 copy-start.4
  322.1 3.3 copy-start.6
  463.3 21.2 %all-to-all-start = ((bf16[32,2,3456]{2,1,0:T(2,128)(2,1)}), bf16[32,2,3456]{2,1,0:T(2,128)(2,1)}, u32[]{:S(2)}, u32[]{:S(2)}) async-start(bf16[32,2,3456]{2,1,0:T(2,128)(2,1)} %reshape.429), calls=%async_computation | async-start | bytes 884736 | tf_op jit(solution)/shard_map/all_to_all | solution.py:174
  509.6 27.2 %all-to-all-start.1 = ((bf16[1,32,4,576]{3,2,0,1:T(4,128)(2,1)}), bf16[1,32,4,576]{3,2,0,1:T(4,128)(2,1)}, u32[]{:S(2)}, u32[]{:S(2)}) async-start(bf16[1,32,4,576]{3,2,0,1:T(4,128)(2,1)} %reshape.420), calls=%async_computation.1 | async-start | bytes 327680 | tf_op jit(solution)/shard_map/all_to_all | solution.py:178
  536.8 424.4 %all-to-all-start.3 = ((bf16[1,32,4,1728]{3,2,0,1:T(4,128)(2,1)}), bf16[1,32,4,1728]{3,2,0,1:T(4,128)(2,1)}, u32[]{:S(2)}, u32[]{:S(2)}) async-start(bf16[1,32,4,1728]{3,2,0,1:T(4,128)(2,1)} %copy.88), calls=%async_computation.3 | async-start | bytes 917504 | tf_op jit(solution)/shard_map/all_to_all | solution.py:198
  544.6 415.0 %all-reduce.4.cloned.1.call-start = ((), (), s32[]{:S(2)}) async-start(), calls=%async_computation.6 | async-start | bytes 184320 | tf_op jit(solution)/shard_map/psum | solution.py:187
  636.1 12.1 %collective-permute-start.6 = (bf16[48,1152]{1,0:T(8,128)(2,1)}, bf16[48,1152]{1,0:T(8,128)(2,1)}, u32[]{:S(2)}, u32[]{:S(2)}) collective-permute-start(bf16[48,1152]{1,0:T(8,128)(2,1)} %fusion), channel_id=1, source_target_pairs={{0,3},{1,128},{2,129},{3,130},{128,131},{129,256},{130,257},{131,2... | collective-permute-start | bytes 331784
  638.1 10.2 %collective-permute-start.5 = (bf16[48,1152]{1,0:T(8,128)(2,1)}, bf16[48,1152]{1,0:T(8,128)(2,1)}, u32[]{:S(2)}, u32[]{:S(2)}) collective-permute-start(bf16[48,1152]{1,0:T(8,128)(2,1)} %fusion), channel_id=1, source_target_pairs={{0,2},{1,3},{2,128},{3,129},{128,130},{129,131},{130,256},{131,257... | collective-permute-start | bytes 331784
  640.3 8.0 collective-permute-start.4
  644.5 3.8 collective-permute-start.7
  963.2 3.9 copy-start.2
  963.2 3.9 copy-start.9
  963.2 3.9 copy-start.13
  967.1 0.7 copy-start.16
  967.8 1.9 copy-start.5
  969.7 1.4 copy-start.8
  979.8 7.1 copy-start.7
  982.0 12.8 %collective-permute-start.2 = (bf16[1,1,64,1152]{2,3,1,0:T(8,128)(2,1)}, bf16[1,1,64,1152]{2,3,1,0:T(8,128)(2,1)}, u32[]{:S(2)}, u32[]{:S(2)}) collective-permute-start(bf16[1,1,64,1152]{2,3,1,0:T(8,128)(2,1)} %get-tuple-element.5), channel_id=1, source_target_pairs={{0,1},{1,2},{2,3},{4,5},{5,6},{6,7},{8,9},{9,10},{10,11},{12,13},{... | collective-permute-start | bytes 442376 | tf_op jit(solution)/shard_map/ppermute | solution.py:30
  985.5 9.4 copy-start.3
  985.5 9.3 collective-permute-start.3
  996.2 3.7 copy-start.10
  996.2 3.7 copy-start.12
  996.2 3.7 copy-start.14
  996.2 3.7 copy-start.15
Sparse Core Ops, SparseCore 0:
  11.0 89.9 all-gather.12
  104.1 128.3 all-gather.6
  235.5 81.2 all-gather.10
  319.7 128.3 all-gather.8
  658.0 301.5 all-reduce.3
where the time goes:
time: 1010 us
  waiting for transfers between devices  707 us (70%)
  blocking collectives  87.2 us (9%)
  local copies, waits for them, and re-layouts  75 us (7%)
  matrix products  61.8 us (6%)
  starting transfers between devices  43.5 us (4%)
  other arithmetic  18.5 us (2%)
  between operations  14.8 us (1%)
    psum x1, waiting for transfers between devices, local(): time_out_grad = lax.psum(rows_part, 'seq').astype(jnp.float32)  300 us
    all_gather x1, waiting for transfers between devices, local(): lax.all_gather(space_qkv, ('dp', 'tile'), axis=0, tiled=True)  129 us
    all_gather x1, waiting for transfers between devices, local(): lax.all_gather(time_qkv, ('dp', 'tile'), axis=0, tiled=True)  118 us
    unnamed x1, blocking collectives  87.2 us
    all_gather x1, waiting for transfers between devices, local(): lax.all_gather(time_out, ('dp', 'tile'), axis=0, tiled=True)  86.8 us
    all_gather x1, waiting for transfers between devices, local(): lax.all_gather(space_out, ('dp', 'tile'), axis=0, tiled=True)  64.3 us
    unnamed x45, local copies, waits for them, and re-layouts  26.8 us
  transfers between devices with their start and end apart: 17, of which 6 were waited for; matrix products, arithmetic and copies ran while one was open for 19% of the time, Pallas kernels for 0%

commit v1 on v0

--- a/solution.py
+++ b/solution.py
@@ -1,6 +1,8 @@
 import jax
 import jax.numpy as jnp
 from jax import lax
+from jax.experimental import pallas as pl
+from jax.experimental.pallas import tpu as pltpu
 from jax.sharding import PartitionSpec as P
 
 HEADS = 8
@@ -124,6 +126,251 @@
 def time_ok(time_mask):
     frame = jnp.arange(time_mask.shape[0])
     return (frame[None, :] == frame[:, None]) | (frame[None, :] < frame[:, None]) & (time_mask == 1)
+
+
+MESH = pl.DeviceIdType.MESH
+LANES = (896, 640, 896)
+
+
+def coords():
+    dp, seq, tile = lax.axis_index("dp"), lax.axis_index("seq"), lax.axis_index("tile")
+    return dp, seq // 8, (seq // 2) % 4, seq % 2, tile
+
+
+def at(dp, y, zl, core, tile):
+    return (dp, (y * 4 + zl) * 2 + core, tile)
+
+
+class Gather:
+    def __init__(self, bufs, send, recv):
+        self.bufs, self.send, self.recv = bufs, send, recv
+        dp, y, zl, core, x = self.pos = coords()
+        self.first = core == 0
+        self.p1 = jnp.where(self.first, y, x)
+        self.p2 = jnp.where(self.first, x, y)
+        self.q2 = jnp.where(self.first, y, x)
+
+    def own(self, g):
+        return self.bufs[g].at[self.pos[3], self.p2, self.p1]
+
+    def along1(self, place):
+        dp, y, zl, core, x = self.pos
+        place = lax.rem(place + 4, 4)
+        return at(dp, jnp.where(self.first, place, y), zl, core, jnp.where(self.first, x, place))
+
+    def along2(self, place):
+        dp, y, zl, core, x = self.pos
+        place = lax.rem(place + 4, 4)
+        return at(dp, jnp.where(self.first, y, place), zl, core, jnp.where(self.first, place, x))
+
+    def copy(self, g, ref, slot, target, recv_slot=None):
+        return pltpu.make_async_remote_copy(
+            src_ref=ref,
+            dst_ref=ref,
+            send_sem=self.send.at[g, slot],
+            recv_sem=self.recv.at[g, slot if recv_slot is None else recv_slot],
+            device_id=target,
+            device_id_type=MESH,
+        )
+
+    def third(self, g, zl):
+        return self.own(g).at[pl.ds(3 * zl, 3)]
+
+    def zsend(self, g):
+        dp, y, zl, core, x = self.pos
+
+        @pl.when((dp == y) & (zl < 3))
+        def _():
+            for k in range(1, 4):
+                self.copy(g, self.third(g, zl), k - 1, at(lax.rem(dp + k, 4), y, zl, core, x), 0).start()
+
+    def zpass(self, g):
+        dp, y, zl, core, x = self.pos
+
+        @pl.when((dp != y) & (zl < 3))
+        def _():
+            self.copy(g, self.third(g, zl), 0, self.pos_id(), 0).wait_recv()
+            for k in range(1, 4):
+                target = at(dp, y, lax.rem(zl + k, 4), core, x)
+                self.copy(g, self.third(g, zl), k - 1, target, 1 + zl).start()
+
+    def pos_id(self):
+        dp, y, zl, core, x = self.pos
+        return at(dp, y, zl, core, x)
+
+    def zdone(self, g):
+        dp, y, zl, core, x = self.pos
+        for source in range(3):
+
+            @pl.when((dp != y) & (zl != source))
+            def _():
+                self.copy(g, self.third(g, source), 0, self.pos_id(), 1 + source).wait_recv()
+
+    def zend(self, g):
+        dp, y, zl, core, x = self.pos
+
+        @pl.when(zl < 3)
+        def _():
+            for k in range(3):
+                self.copy(g, self.third(g, zl), k, self.pos_id()).wait_send()
+
+    def one(self, g, place):
+        return self.bufs[g].at[self.pos[3], self.p2, lax.rem(place + 4, 4)]
+
+    def bundle(self, g, place):
+        return self.bufs[g].at[self.pos[3], lax.rem(place + 4, 4)]
+
+    def ring_send(self, g, part, along, p, slot):
+        self.copy(g, part(g, p), slot, along(p + 1)).start()
+        self.copy(g, part(g, p), slot + 1, along(p - 1)).start()
+
+    def ring_pass(self, g, part, along, p, slot, cut, size):
+        low, high = pl.ds(0, cut), pl.ds(cut, size - cut)
+        self.copy(g, part(g, p - 1), slot, along(p)).wait_recv()
+        self.copy(g, part(g, p - 1).at[low], slot + 2, along(p + 1)).start()
+        self.copy(g, part(g, p + 1), slot + 1, along(p)).wait_recv()
+        self.copy(g, part(g, p + 1).at[high], slot + 3, along(p - 1)).start()
+
+    def ring_done(self, g, part, along, p, slot, cut, size):
+        low, high = pl.ds(0, cut), pl.ds(cut, size - cut)
+        self.copy(g, part(g, p + 2).at[low], slot + 2, along(p)).wait_recv()
+        self.copy(g, part(g, p + 2).at[high], slot + 3, along(p)).wait_recv()
+
+    def ring_end(self, g, part, along, p, slot, cut, size):
+        low, high = pl.ds(0, cut), pl.ds(cut, size - cut)
+        self.copy(g, part(g, p), slot, along(p)).wait_send()
+        self.copy(g, part(g, p), slot + 1, along(p)).wait_send()
+        self.copy(g, part(g, p - 1).at[low], slot + 2, along(p)).wait_send()
+        self.copy(g, part(g, p + 1).at[high], slot + 3, along(p)).wait_send()
+
+    def s1send(self, g):
+        self.zdone(g)
+        self.ring_send(g, self.one, self.along1, self.p1, 4)
+
+    def s1pass(self, g):
+        self.ring_pass(g, self.one, self.along1, self.p1, 4, 5, 9)
+
+    def s2send(self, g):
+        self.ring_done(g, self.one, self.along1, self.p1, 4, 5, 9)
+        self.ring_send(g, self.bundle, self.along2, self.p2, 8)
+        self.twin(g, 0)
+
+    def s2pass(self, g):
+        self.ring_pass(g, self.bundle, self.along2, self.p2, 8, 2, 4)
+        self.twin(g, -1)
+        self.twin(g, 1)
+
+    def s2done(self, g):
+        self.ring_done(g, self.bundle, self.along2, self.p2, 8, 2, 4)
+        self.twin(g, 2)
+
+    def twin(self, g, step):
+        dp, y, zl, core, x = self.pos
+        self.copy(g, self.bundle(g, self.p2 + step), 13 + step, at(dp, y, zl, 1 - core, x)).start()
+
+    def end(self, g):
+        dp, y, zl, core, x = self.pos
+        for step in (0, -1, 1, 2):
+            ref = self.bufs[g].at[1 - core, lax.rem(self.q2 + step + 4, 4)]
+            self.copy(g, ref, 13 + step, self.pos_id()).wait_recv()
+
+    def drain(self, g):
+        self.zend(g)
+        self.ring_end(g, self.one, self.along1, self.p1, 4, 5, 9)
+        self.ring_end(g, self.bundle, self.along2, self.p2, 8, 2, 4)
+        for step in (0, -1, 1, 2):
+            self.copy(g, self.bundle(g, self.p2 + step), 13 + step, self.pos_id()).wait_send()
+
+
+def greet():
+    dp, y, zl, core, x = coords()
+    barrier = pltpu.get_barrier_semaphore()
+    others = [at(lax.rem(dp + k, 4), y, zl, core, x) for k in range(1, 4)]
+    others += [at(dp, lax.rem(y + k, 4), zl, core, x) for k in range(1, 4)]
+    others += [at(dp, y, lax.rem(zl + k, 4), core, x) for k in range(1, 4)]
+    others += [at(dp, y, zl, core, lax.rem(x + k, 4)) for k in range(1, 4)]
+    others += [at(dp, y, zl, 1 - core, x)]
+    for target in others:
+        pl.semaphore_signal(barrier, inc=1, device_id=target, device_id_type=MESH)
+    pl.semaphore_wait(barrier, len(others))
+
+
+def place_own(gather, space_qkv, space_out, time_qkv, time_out):
+    dp, y, zl, core, x = gather.pos
+    for half in range(2):
+
+        @pl.when((dp == y) & (core == half))
+        def _():
+            for g, ref in ((0, space_qkv), (2, time_qkv)):
+                if half == 0:
+                    block = ref[:, :896]
+                else:
+                    block = jnp.concatenate([ref[:, 896:], jnp.zeros((72, 64), jnp.bfloat16)], axis=1)
+                gather.own(g)[...] = block.reshape(9, 8, 896)
+            block = jnp.concatenate(
+                [space_out[...].astype(jnp.float32), time_out[...].astype(jnp.float32)], axis=0
+            )
+            if half == 0:
+                block = block[:, :640]
+            else:
+                block = jnp.concatenate([block[:, 640:], jnp.zeros((72, 128), jnp.float32)], axis=1)
+            gather.own(1)[...] = block.astype(jnp.bfloat16).reshape(9, 8, 640)
+
+
+def gather_kernel(space_qkv, space_out, time_qkv, time_out, w0, w1, w2, send, recv):
+    gather = Gather((w0, w1, w2), send, recv)
+    place_own(gather, space_qkv, space_out, time_qkv, time_out)
+    greet()
+    for g in range(3):
+        gather.zsend(g)
+    gather.zpass(0)
+    gather.s1send(0)
+    gather.zpass(1)
+    gather.s1pass(0)
+    gather.s2send(0)
+    gather.s1send(1)
+    gather.zpass(2)
+    gather.s1pass(1)
+    gather.s2pass(0)
+    gather.s2send(1)
+    gather.s1send(2)
+    gather.s2done(0)
+    gather.s1pass(2)
+    gather.s2pass(1)
+    gather.s2send(2)
+    gather.s2done(1)
+    gather.s2pass(2)
+    gather.s2done(2)
+    for g in range(3):
+        gather.end(g)
+    for g in range(3):
+        gather.drain(g)
+
+
+def gathered(space_qkv, space_out, time_qkv, time_out):
+    w0, w1, w2 = pl.pallas_call(
+        gather_kernel,
+        out_shape=[jax.ShapeDtypeStruct((2, 4, 4, 9, 8, lanes), jnp.bfloat16) for lanes in LANES],
+        in_specs=[pl.BlockSpec(memory_space=pltpu.VMEM)] * 4,
+        out_specs=[pl.BlockSpec(memory_space=pltpu.VMEM)] * 3,
+        scratch_shapes=[pltpu.SemaphoreType.DMA((3, 16)), pltpu.SemaphoreType.DMA((3, 16))],
+        compiler_params=pltpu.CompilerParams(
+            collective_id=0, has_side_effects=True, vmem_limit_bytes=60 << 20
+        ),
+    )(space_qkv, space_out, time_qkv, time_out)
+
+    def whole(buf):
+        lanes = buf.shape[-1]
+        first = buf[0].transpose(1, 0, 2, 3, 4).reshape(1152, lanes)
+        return jnp.concatenate([first, buf[1].reshape(1152, lanes)], axis=1)
+
+    outs = whole(w1)[:, :1152].reshape(16, 72, 1152)
+    return (
+        whole(w0)[:, :1728],
+        outs[:, :36].reshape(576, 1152),
+        whole(w2)[:, :1728],
+        outs[:, 36:].reshape(576, 1152),
+    )
 
 
 def local(
@@ -140,9 +387,8 @@
     width = HEADS * HEAD_DIM
     own = latents.shape[2]
     span = own // 2
-    space_qkv_all, space_out_all = (
-        lax.all_gather(space_qkv, ("dp", "tile"), axis=0, tiled=True),
-        lax.all_gather(space_out, ("dp", "tile"), axis=0, tiled=True),
+    space_qkv_all, space_out_all, time_qkv_all, time_out_all = gathered(
+        space_qkv, space_out, time_qkv, time_out
     )
     start = latents.astype(jnp.float32)
     gain_space = 1.0 + modulation[:, 0][:, None, None, :]
@@ -163,10 +409,6 @@
     space_heads, space_probs = attend(query, keys, values, allowed, True)
     space_att = merged(space_heads)
     middle = start + project(space_att, space_out_all)
-    time_qkv_all, time_out_all = (
-        lax.all_gather(time_qkv, ("dp", "tile"), axis=0, tiled=True),
-        lax.all_gather(time_out, ("dp", "tile"), axis=0, tiled=True),
-    )
     inverse_time, normed_time = norm_scale(middle, gain_time)
     normed_time = normed_time.astype(jnp.bfloat16)
     frame_mask = time_ok(time_mask)[None, None, None]

time: 1010 us -> 701 us (0.69)
  waiting for transfers between devices: 707 us -> 282 us
  Pallas kernels: 0 us -> 84 us
  starting transfers between devices: 43.5 us -> 56.6 us
    all_gather x4 -> x0, waiting for transfers between devices: 399 us -> none  [the longest x1 129 us: local(): lax.all_gather(space_qkv, ('dp', 'tile'), axis=0, tiled=True)]
    pallas_call x0 -> x1, Pallas kernels: none -> 84 us  [gathered(): pl.pallas_call(gather_kernel, out_shape=[jax.ShapeDtypeStruct((2, 4, 4, 9...]
    psum x1, waiting for transfers between devices: 300 us -> 275 us  [local(): time_out_grad = lax.psum(rows_part, 'seq').astype(jnp.float32)]
    unnamed x45 -> x73, local copies, waits for them, and re-layouts: 26.8 us -> 25 us
  transfers between devices with their start and end apart: 17 -> 13, of which waited for: 6 -> 2; matrix products, arithmetic and copies ran while one was open for 19% -> 28% of each run, Pallas kernels for 0% -> 0%
where the time goes in v1:
time: 701 us; the launch traced here: 690 us
  waiting for transfers between devices  282 us (40%)
  blocking collectives  95.9 us (14%)
  Pallas kernels  84 us (12%)
  local copies, waits for them, and re-layouts  84 us (12%)
  matrix products  57.4 us (8%)
  starting transfers between devices  56.6 us (8%)
  between operations  15.4 us (2%)
  other arithmetic  14.4 us (2%)
    psum x1, waiting for transfers between devices, local(): time_out_grad = lax.psum(rows_part, 'seq').astype(jnp.float32)  275 us
    unnamed x1, blocking collectives  95.9 us
    pallas_call x1, Pallas kernels, gathered(): pl.pallas_call(gather_kernel, out_shape=[jax.ShapeDtypeStruct((2, 4, 4, 9...  84 us
    unnamed x73, local copies, waits for them, and re-layouts  25 us
    unnamed x4, starting transfers between devices  16.6 us
  transfers between devices with their start and end apart: 13, of which 2 were waited for; matrix products, arithmetic and copies ran while one was open for 28% of the time, Pallas kernels for 0%

profile of v1, /device:TPU:1, one launch (start us, length us, event | category | flops | bytes accessed | tf_op | source)
XLA Modules:
  0.0 689.6 jit_solution(2251350342540445925)
XLA Ops:
  7.2 84.0 %shard_map.112 = (bf16[2,4,4,9,8,896]{5,4,3,2,1,0:T(8,128)(2,1)}, bf16[2,4,4,9,8,640]{5,4,3,2,1,0:T(8,128)(2,1)}, bf16[2,4,4,9,8,896]{5,4,3,2,1,0:T(8,128)(2,1)}) custom-call(bf16[72,1728]{1,0:T(8,128)(2,1)} %space_qkv.1, bf16[36,1152]{1,0:T(8,128)(2,1)} %space_out.1, bf16[72,1728]{1,0:T(8,128)(2,1)} %time_qkv.1, bf16[36,1152]{1,0:T(8,128)(2,1)} %time_out.1), custom_call_target="tpu_custom_call" | custom-call | tf_op jit(solution)/shard_map/pallas_call | solution.py:351
  91.2 5.1 slice_bitcast_fusion
  100.8 4.0 collective-permute-start
  113.0 10.1 %all-to-all-start.2 = ((bf16[32,2,1152]{2,1,0:T(2,128)(2,1)}), bf16[32,2,1152]{2,1,0:T(2,128)(2,1)}, u32[]{:S(2)}, u32[]{:S(2)}) async-start(bf16[32,2,1152]{2,1,0:T(2,128)(2,1)} %reshape.451), calls=%async_computation.2 | async-start | bytes 294912 | tf_op jit(solution)/shard_map/all_to_all | solution.py:431
  124.9 2.2 reshape.422
  127.1 3.1 copy.75
  131.7 2.7 fusion.117
  134.4 2.4 convolution_convert_fusion.6
  139.6 4.0 fusion.16
  143.7 3.1 copy.76
  146.7 5.3 reduce.24
  152.0 2.3 reshape.449
  154.3 8.4 %all-to-all-start = ((bf16[32,2,3456]{2,1,0:T(2,128)(2,1)}), bf16[32,2,3456]{2,1,0:T(2,128)(2,1)}, u32[]{:S(2)}, u32[]{:S(2)}) async-start(bf16[32,2,3456]{2,1,0:T(2,128)(2,1)} %reshape.449), calls=%async_computation | async-start | bytes 884736 | tf_op jit(solution)/shard_map/all_to_all | solution.py:416
  164.1 2.2 reshape.452
  166.3 2.6 bitcast_reduce_fusion.1
  168.8 1.9 reshape.434
  170.7 6.9 %all-to-all-done = bf16[32,2,3456]{2,1,0:T(2,128)(2,1)} async-done(((bf16[32,2,3456]{2,1,0:T(2,128)(2,1)}), bf16[32,2,3456]{2,1,0:T(2,128)(2,1)}, u32[]{:S(2)}, u32[]{:S(2)}) %all-to-all-start) | async-done | bytes 442400 | tf_op jit(solution)/shard_map/all_to_all | solution.py:416
  177.7 3.9 reshape.450
  181.6 4.6 bitcast_reduce_fusion
  186.1 1.9 all_to_all.11
  188.0 2.0 fusion.115
  190.1 1.9 reshape.443
  192.0 1.9 reshape.444
  194.0 1.9 reshape.442
  195.9 2.8 fusion.118
  200.9 1.9 reshape.440
  202.8 4.4 all-to-all-start.1
  209.4 1.9 concatenate.56
  211.3 2.1 fusion.87
  213.4 2.7 fusion.35
  219.7 2.7 fusion.34
  226.1 2.0 concatenate.57
  228.1 2.2 copy.97
  230.3 7.8 %all-to-all-start.3 = ((bf16[1,32,4,1728]{3,2,0,1:T(4,128)(2,1)}), bf16[1,32,4,1728]{3,2,0,1:T(4,128)(2,1)}, u32[]{:S(2)}, u32[]{:S(2)}) async-start(bf16[1,32,4,1728]{3,2,0,1:T(4,128)(2,1)} %copy.97), calls=%async_computation.3 | async-start | bytes 917504 | tf_op jit(solution)/shard_map/all_to_all | solution.py:440
  239.7 2.6 convolution_convert_fusion
  242.3 95.9 %fusion = bf16[48,1152]{1,0:T(8,128)(2,1)} fusion(bf16[576,1152]{1,0:T(8,128)(2,1)} %convolution_convert_fusion), kind=kCustom, calls=%all-reduce-scatter | all-reduce-scatter fusion | flops 884737 | bytes 1439744
  338.2 1.9 collective-permute-start.4
  340.1 2.5 collective-permute-start.5
  342.6 9.0 %collective-permute-start.6 = (bf16[48,1152]{1,0:T(8,128)(2,1)}, bf16[48,1152]{1,0:T(8,128)(2,1)}, u32[]{:S(2)}, u32[]{:S(2)}) collective-permute-start(bf16[48,1152]{1,0:T(8,128)(2,1)} %fusion), channel_id=1, source_target_pairs={{0,3},{1,128},{2,129},{3,130},{128,131},{129,256},{130,257},{131,2... | collective-permute-start | bytes 331784
  353.1 3.2 collective-permute-start.7
  358.2 8.0 %concatenate.64 = bf16[228,1152]{1,0:T(8,128)(2,1)} concatenate(bf16[36,1152]{1,0:T(8,128)(2,1)} %collective-permute-done.7, bf16[48,1152]{1,0:T(8,128)(2,1)} %collective-permute-done.6, bf16[48,1152]{1,0:T(8,128)(2,1)} %collective-permute-done.5, bf16[48,1152]{1,0:T(8,128)(2,1)} %collective-permute-done.4, bf16[48,1152]{1,0:T(8,128)(2,1)} %fusion), dimensions={0} | concatenate | bytes 1050624
  367.9 2.0 fusion.13
  369.9 275.0 %all-reduce.4.cloned.1.call-done = bf16[36,1152]{1,0:T(8,128)(2,1)} async-done(((bf16[36,1152]{1,0:T(8,128)(2,1)}), bf16[36,1152]{1,0:T(8,128)(2,1)}) %all-reduce.4.cloned.1.call-update) | async-done | bytes 82960 | tf_op jit(solution)/shard_map/psum | solution.py:429
  647.7 3.7 fusion.58
  655.8 7.7 %fusion.38 = f32[8,72,256]{2,1,0:T(8,128)S(1)} fusion(bf16[128,8,72]{0,2,1:T(8,128)(2,1)S(1)} %bitcast.189, f32[8,128,256]{2,1,0:T(8,128)} %fusion.123, f32[8,128,256]{2,1,0:T(8,128)} %get-tuple-element.33, f32[8,128]{1,0:T(8,128)S(1)} %copy-done.31), kind=kOutput, calls=%fused_computation.63 | convolution fusion | flops 39585024 | bytes 2838528 | tf_op jit(solution)/shard_map/cbhqk,cbqhe->cbkhe/dot_general | solution.py:114
  664.5 2.8 collective-permute-start.2
  668.6 7.7 %convolution_convert_fusion.5 = bf16[8,72,128]{2,1,0:T(8,128)(2,1)S(1)} fusion(bf16[256,8,72]{0,2,1:T(8,128)(2,1)S(1)} %bitcast.184, f32[8,128,256]{2,1,0:T(8,128)} %fusion.123, f32[8,128,256]{2,1,0:T(8,128)} %get-tuple-element.33, f32[8,128]{1,0:T(8,128)S(1)} %copy-done.31), kind=kOutput, calls=%fused_computation.58 | convolution fusion | flops 39658752 | bytes 2543616 | tf_op jit(solution)/shard_map/cbhqk,cbkhe->cbqhe/dot_general | solution.py:111
  677.7 3.8 fusion.54
  (135 shorter events, 49.5 us)
Async XLA Ops:
  96.3 1.9 copy-start.10
  96.3 0.7 copy-start.17
  96.3 1.2 copy-start.2
  97.0 2.8 copy-start.8
  97.5 2.4 copy-start.18
  97.5 41.6 %copy-start.20 = (f32[1152]{0:T(1024)}, f32[1152]{0:T(1024)S(1)}, u32[]{:S(2)}) copy-start(f32[1152]{0:T(1024)S(1)} %get-tuple-element.9) | copy-start | bytes 13828
  98.2 1.7 copy-start.27
  98.2 8.0 %copy-start.1 = (bf16[2,4,4,9,8,640]{5,4,3,2,1,0:T(8,128)(2,1)S(1)}, bf16[2,4,4,9,8,640]{5,4,3,2,1,0:T(8,128)(2,1)}, u32[]{:S(2)}) copy-start(bf16[2,4,4,9,8,640]{5,4,3,2,1,0:T(8,128)(2,1)} %get-tuple-element.7) | copy-start | bytes 8847364
  99.9 6.5 copy-start.4
  100.8 29.4 %collective-permute-start = (bf16[1,1,64,1152]{2,3,1,0:T(8,128)(2,1)}, bf16[1,1,64,1152]{2,3,1,0:T(8,128)(2,1)}, u32[]{:S(2)}, u32[]{:S(2)}) collective-permute-start(bf16[1,1,64,1152]{2,3,1,0:T(8,128)(2,1)} %get-tuple-element.26), channel_id=1, source_target_pairs={{0,1},{1,2},{2,3},{4,5},{5,6},{6,7},{8,9},{9,10},{10,11},{12,13},{... | collective-permute-start | bytes 442376 | tf_op jit(solution)/shard_map/ppermute | solution.py:21
  104.8 25.4 %collective-permute-start.1 = (bf16[1,1,64,1152]{2,3,1,0:T(8,128)(2,1)}, bf16[1,1,64,1152]{2,3,1,0:T(8,128)(2,1)}, u32[]{:S(2)}, u32[]{:S(2)}) collective-permute-start(bf16[1,1,64,1152]{2,3,1,0:T(8,128)(2,1)} %get-tuple-element.27), channel_id=1, source_target_pairs={{1,0},{2,1},{3,2},{5,4},{6,5},{7,6},{9,8},{10,9},{11,10},{13,12},{... | collective-permute-start | bytes 442376 | tf_op jit(solution)/shard_map/ppermute | solution.py:24
  108.3 1.0 copy-start
  109.2 13.9 %copy-start.5 = (bf16[1,1,128,1728]{2,3,1,0:T(8,128)(2,1)S(1)}, bf16[1,1,128,1728]{2,3,1,0:T(8,128)(2,1)}, u32[]{:S(2)}) copy-start(bf16[1,1,128,1728]{2,3,1,0:T(8,128)(2,1)} %copy-done.4) | copy-start | bytes 1327108
  109.2 14.6 %copy-start.25 = (s32[2,4]{1,0:T(2,128)S(1)}, s32[2,4]{1,0:T(2,128)}, u32[]{:S(2)}) copy-start(s32[2,4]{1,0:T(2,128)} %param.16) | copy-start | bytes 100
  113.0 41.3 %all-to-all-start.2 = ((bf16[32,2,1152]{2,1,0:T(2,128)(2,1)}), bf16[32,2,1152]{2,1,0:T(2,128)(2,1)}, u32[]{:S(2)}, u32[]{:S(2)}) async-start(bf16[32,2,1152]{2,1,0:T(2,128)(2,1)} %reshape.451), calls=%async_computation.2 | async-start | bytes 294912 | tf_op jit(solution)/shard_map/all_to_all | solution.py:431
  127.1 3.1 slice-start
  131.7 5.1 copy-start.11
  131.7 5.1 copy-start.13
  134.4 2.4 copy-start.30
  136.8 2.8 copy-start.9
  139.1 0.5 copy-start.23
  143.7 19.1 %copy-start.16 = (s32[32,32]{1,0:T(8,128)S(1)}, s32[32,32]{1,0:T(8,128)}, u32[]{:S(2)}) copy-start(s32[32,32]{1,0:T(8,128)} %param.17) | copy-start | bytes 12292
  154.3 23.3 %all-to-all-start = ((bf16[32,2,3456]{2,1,0:T(2,128)(2,1)}), bf16[32,2,3456]{2,1,0:T(2,128)(2,1)}, u32[]{:S(2)}, u32[]{:S(2)}) async-start(bf16[32,2,3456]{2,1,0:T(2,128)(2,1)} %reshape.449), calls=%async_computation | async-start | bytes 884736 | tf_op jit(solution)/shard_map/all_to_all | solution.py:416
  198.6 8.5 %copy-start.29 = (f32[4,8,32]{2,1,0:T(8,128)S(1)}, f32[4,8,32]{2,1,0:T(8,128)}, u32[]{:S(2)}) copy-start(f32[4,8,32]{2,1,0:T(8,128)} %get-tuple-element.36) | copy-start | bytes 12292
  202.8 27.5 %all-to-all-start.1 = ((bf16[1,32,4,576]{3,2,0,1:T(4,128)(2,1)}), bf16[1,32,4,576]{3,2,0,1:T(4,128)(2,1)}, u32[]{:S(2)}, u32[]{:S(2)}) async-start(bf16[1,32,4,576]{3,2,0,1:T(4,128)(2,1)} %reshape.440), calls=%async_computation.1 | async-start | bytes 327680 | tf_op jit(solution)/shard_map/all_to_all | solution.py:420
  230.3 416.2 %all-to-all-start.3 = ((bf16[1,32,4,1728]{3,2,0,1:T(4,128)(2,1)}), bf16[1,32,4,1728]{3,2,0,1:T(4,128)(2,1)}, u32[]{:S(2)}, u32[]{:S(2)}) async-start(bf16[1,32,4,1728]{3,2,0,1:T(4,128)(2,1)} %copy.97), calls=%async_computation.3 | async-start | bytes 917504 | tf_op jit(solution)/shard_map/all_to_all | solution.py:440
  238.0 406.8 %all-reduce.4.cloned.1.call-start = ((), (), s32[]{:S(2)}) async-start(), calls=%async_computation.4 | async-start | bytes 184320 | tf_op jit(solution)/shard_map/psum | solution.py:429
  338.2 20.0 %collective-permute-start.4 = (bf16[48,1152]{1,0:T(8,128)(2,1)}, bf16[48,1152]{1,0:T(8,128)(2,1)}, u32[]{:S(2)}, u32[]{:S(2)}) collective-permute-start(bf16[48,1152]{1,0:T(8,128)(2,1)} %fusion), channel_id=1, source_target_pairs={{0,1},{1,2},{2,3},{3,128},{128,129},{129,130},{130,131},{131,256},... | collective-permute-start | bytes 331784
  340.1 18.1 %collective-permute-start.5 = (bf16[48,1152]{1,0:T(8,128)(2,1)}, bf16[48,1152]{1,0:T(8,128)(2,1)}, u32[]{:S(2)}, u32[]{:S(2)}) collective-permute-start(bf16[48,1152]{1,0:T(8,128)(2,1)} %fusion), channel_id=1, source_target_pairs={{0,2},{1,3},{2,128},{3,129},{128,130},{129,131},{130,256},{131,257... | collective-permute-start | bytes 331784
  342.6 15.6 %collective-permute-start.6 = (bf16[48,1152]{1,0:T(8,128)(2,1)}, bf16[48,1152]{1,0:T(8,128)(2,1)}, u32[]{:S(2)}, u32[]{:S(2)}) collective-permute-start(bf16[48,1152]{1,0:T(8,128)(2,1)} %fusion), channel_id=1, source_target_pairs={{0,3},{1,128},{2,129},{3,130},{128,131},{129,256},{130,257},{131,2... | collective-permute-start | bytes 331784
  353.1 5.0 collective-permute-start.7
  366.2 281.4 %copy-start.21 = (f32[1152]{0:T(1024)S(1)}, f32[1152]{0:T(1024)}, u32[]{:S(2)}) copy-start(f32[1152]{0:T(1024)} %copy-done.20) | copy-start | bytes 13828
  647.7 3.8 copy-start.22
  647.7 3.8 copy-start.24
  651.4 2.5 copy-start.6
  651.4 1.2 copy-start.12
  651.4 2.4 copy-start.31
  653.9 1.9 copy-start.15
  663.5 5.1 copy-start.14
  664.5 11.9 %collective-permute-start.2 = (bf16[1,1,64,1152]{2,3,1,0:T(8,128)(2,1)}, bf16[1,1,64,1152]{2,3,1,0:T(8,128)(2,1)S(1)}, u32[]{:S(2)}, u32[]{:S(2)}) collective-permute-start(bf16[1,1,64,1152]{2,3,1,0:T(8,128)(2,1)} %get-tuple-element.19), channel_id=1, source_target_pairs={{0,1},{1,2},{2,3},{4,5},{5,6},{6,7},{8,9},{9,10},{10,11},{12,13},{... | collective-permute-start | bytes 442376 | tf_op jit(solution)/shard_map/ppermute | solution.py:32
  667.3 9.1 %collective-permute-start.3 = (bf16[1,1,64,1152]{2,3,1,0:T(8,128)(2,1)S(1)}, bf16[1,1,64,1152]{2,3,1,0:T(8,128)(2,1)}, u32[]{:S(2)}, u32[]{:S(2)}) collective-permute-start(bf16[1,1,64,1152]{2,3,1,0:T(8,128)(2,1)S(1)} %get-tuple-element.20), channel_id=1, source_target_pairs={{1,0},{2,1},{3,2},{5,4},{6,5},{7,6},{9,8},{10,9},{11,10},{13,12},{... | collective-permute-start | bytes 442376 | tf_op jit(solution)/shard_map/ppermute | solution.py:32
  676.3 1.3 copy-start.3
  676.3 1.3 copy-start.19
  677.7 3.8 copy-start.7
  677.7 3.8 copy-start.26
  677.7 3.8 copy-start.28
Sparse Core Ops, SparseCore 0:
  368.0 276.8 all-reduce.3

commit v2 on v1

v2 whole, which is shorter than its diff:
```python
import jax
import jax.numpy as jnp
from jax import lax
from jax.experimental import pallas as pl
from jax.experimental.pallas import tpu as pltpu
from jax.sharding import PartitionSpec as P

HEADS = 8
HEAD_DIM = 72
WIDTH = HEADS * HEAD_DIM
WIDE = 640
D = 1152
ROWS = 128
EPSILON = 1e-06
MASKED = -1e30
SCALE = HEAD_DIM ** (-0.5)
BF16 = jnp.bfloat16
F32 = jnp.float32

MESH = pl.DeviceIdType.MESH
LANES = (896, 640, 896)


def coords():
    dp, seq, tile = lax.axis_index("dp"), lax.axis_index("seq"), lax.axis_index("tile")
    return dp, seq // 8, (seq // 2) % 4, seq % 2, tile


def at(dp, y, zl, core, tile):
    return (dp, (y * 4 + zl) * 2 + core, tile)


class Gather:
    def __init__(self, bufs, send, recv):
        self.bufs, self.send, self.recv = bufs, send, recv
        dp, y, zl, core, x = self.pos = coords()
        self.first = core == 0
        self.p1 = jnp.where(self.first, y, x)
        self.p2 = jnp.where(self.first, x, y)
        self.q2 = jnp.where(self.first, y, x)

    def own(self, g):
        return self.bufs[g].at[self.pos[3], self.p2, self.p1]

    def along1(self, place):
        dp, y, zl, core, x = self.pos
        place = lax.rem(place + 4, 4)
        return at(dp, jnp.where(self.first, place, y), zl, core, jnp.where(self.first, x, place))

    def along2(self, place):
        dp, y, zl, core, x = self.pos
        place = lax.rem(place + 4, 4)
        return at(dp, jnp.where(self.first, y, place), zl, core, jnp.where(self.first, place, x))

    def copy(self, g, ref, slot, target, recv_slot=None):
        return pltpu.make_async_remote_copy(
            src_ref=ref,
            dst_ref=ref,
            send_sem=self.send.at[g, slot],
            recv_sem=self.recv.at[g, slot if recv_slot is None else recv_slot],
            device_id=target,
            device_id_type=MESH,
        )

    def third(self, g, zl):
        return self.own(g).at[pl.ds(3 * zl, 3)]

    def zsend(self, g):
        dp, y, zl, core, x = self.pos

        @pl.when((dp == y) & (zl < 3))
        def _():
            for k in range(1, 4):
                self.copy(g, self.third(g, zl), k - 1, at(lax.rem(dp + k, 4), y, zl, core, x), 0).start()

    def zpass(self, g):
        dp, y, zl, core, x = self.pos

        @pl.when((dp != y) & (zl < 3))
        def _():
            self.copy(g, self.third(g, zl), 0, self.pos_id(), 0).wait_recv()
            for k in range(1, 4):
                target = at(dp, y, lax.rem(zl + k, 4), core, x)
                self.copy(g, self.third(g, zl), k - 1, target, 1 + zl).start()

    def pos_id(self):
        dp, y, zl, core, x = self.pos
        return at(dp, y, zl, core, x)

    def zdone(self, g):
        dp, y, zl, core, x = self.pos
        for source in range(3):

            @pl.when((dp != y) & (zl != source))
            def _():
                self.copy(g, self.third(g, source), 0, self.pos_id(), 1 + source).wait_recv()

    def zend(self, g):
        dp, y, zl, core, x = self.pos

        @pl.when(zl < 3)
        def _():
            for k in range(3):
                self.copy(g, self.third(g, zl), k, self.pos_id()).wait_send()

    def one(self, g, place):
        return self.bufs[g].at[self.pos[3], self.p2, lax.rem(place + 4, 4)]

    def bundle(self, g, place):
        return self.bufs[g].at[self.pos[3], lax.rem(place + 4, 4)]

    def ring_send(self, g, part, along, p, slot):
        self.copy(g, part(g, p), slot, along(p + 1)).start()
        self.copy(g, part(g, p), slot + 1, along(p - 1)).start()

    def ring_pass(self, g, part, along, p, slot, cut, size):
        low, high = pl.ds(0, cut), pl.ds(cut, size - cut)
        self.copy(g, part(g, p - 1), slot, along(p)).wait_recv()
        self.copy(g, part(g, p - 1).at[low], slot + 2, along(p + 1)).start()
        self.copy(g, part(g, p + 1), slot + 1, along(p)).wait_recv()
        self.copy(g, part(g, p + 1).at[high], slot + 3, along(p - 1)).start()

    def ring_done(self, g, part, along, p, slot, cut, size):
        low, high = pl.ds(0, cut), pl.ds(cut, size - cut)
        self.copy(g, part(g, p + 2).at[low], slot + 2, along(p)).wait_recv()
        self.copy(g, part(g, p + 2).at[high], slot + 3, along(p)).wait_recv()

    def ring_end(self, g, part, along, p, slot, cut, size):
        low, high = pl.ds(0, cut), pl.ds(cut, size - cut)
        self.copy(g, part(g, p), slot, along(p)).wait_send()
        self.copy(g, part(g, p), slot + 1, along(p)).wait_send()
        self.copy(g, part(g, p - 1).at[low], slot + 2, along(p)).wait_send()
        self.copy(g, part(g, p + 1).at[high], slot + 3, along(p)).wait_send()

    def s1send(self, g):
        self.zdone(g)
        self.ring_send(g, self.one, self.along1, self.p1, 4)

    def s1pass(self, g):
        self.ring_pass(g, self.one, self.along1, self.p1, 4, 5, 9)

    def s2send(self, g):
        self.ring_done(g, self.one, self.along1, self.p1, 4, 5, 9)
        self.ring_send(g, self.bundle, self.along2, self.p2, 8)
        self.twin(g, 0)

    def s2pass(self, g):
        self.ring_pass(g, self.bundle, self.along2, self.p2, 8, 2, 4)
        self.twin(g, -1)
        self.twin(g, 1)

    def s2done(self, g):
        self.ring_done(g, self.bundle, self.along2, self.p2, 8, 2, 4)
        self.twin(g, 2)

    def twin(self, g, step):
        dp, y, zl, core, x = self.pos
        self.copy(g, self.bundle(g, self.p2 + step), 13 + step, at(dp, y, zl, 1 - core, x)).start()

    def end(self, g):
        dp, y, zl, core, x = self.pos
        for step in (0, -1, 1, 2):
            ref = self.bufs[g].at[1 - core, lax.rem(self.q2 + step + 4, 4)]
            self.copy(g, ref, 13 + step, self.pos_id()).wait_recv()

    def drain(self, g):
        self.zend(g)
        self.ring_end(g, self.one, self.along1, self.p1, 4, 5, 9)
        self.ring_end(g, self.bundle, self.along2, self.p2, 8, 2, 4)
        for step in (0, -1, 1, 2):
            self.copy(g, self.bundle(g, self.p2 + step), 13 + step, self.pos_id()).wait_send()


def greet():
    dp, y, zl, core, x = coords()
    barrier = pltpu.get_barrier_semaphore()
    others = [at(lax.rem(dp + k, 4), y, zl, core, x) for k in range(1, 4)]
    others += [at(dp, lax.rem(y + k, 4), zl, core, x) for k in range(1, 4)]
    others += [(dp, y * 8 + lax.rem(zl * 2 + core + k, 8), x) for k in range(1, 8)]
    others += [at(dp, y, zl, core, lax.rem(x + k, 4)) for k in range(1, 4)]
    for target in others:
        pl.semaphore_signal(barrier, inc=1, device_id=target, device_id_type=MESH)
    pl.semaphore_wait(barrier, len(others))


def place_own(gather, space_qkv, space_out, time_qkv, time_out):
    dp, y, zl, core, x = gather.pos
    for half in range(2):

        @pl.when((dp == y) & (core == half))
        def _():
            for g, ref in ((0, space_qkv), (2, time_qkv)):
                if half == 0:
                    block = ref[:, :896]
                else:
                    block = jnp.concatenate([ref[:, 896:], jnp.zeros((72, 64), jnp.bfloat16)], axis=1)
                gather.own(g)[...] = block.reshape(9, 8, 896)
            block = jnp.concatenate(
                [space_out[...].astype(jnp.float32), time_out[...].astype(jnp.float32)], axis=0
            )
            if half == 0:
                block = block[:, :640]
            else:
                block = jnp.concatenate([block[:, 640:], jnp.zeros((72, 128), jnp.float32)], axis=1)
            gather.own(1)[...] = block.astype(jnp.bfloat16).reshape(9, 8, 640)

def rem4(value):
    return lax.rem(value + 4, 4)


class Exchange:
    def __init__(self, n, me, target, block, slot, send, recv):
        self.n, self.me, self.target = n, me, target
        self.block, self.slot, self.sems = block, slot, (send, recv)

    def copy(self, k, src, dst, target):
        return pltpu.make_async_remote_copy(
            src_ref=src,
            dst_ref=dst,
            send_sem=self.sems[0].at[k - 1],
            recv_sem=self.sems[1].at[k - 1],
            device_id=target,
            device_id_type=MESH,
        )

    def start(self):
        for k in range(1, self.n):
            other = lax.rem(self.me + k, self.n)
            self.copy(k, self.block(other), self.slot(self.me), self.target(other)).start()

    def wait(self):
        for k in range(1, self.n):
            source = lax.rem(self.me + self.n - k, self.n)
            self.copy(k, self.slot(source), self.slot(source), self.target(source)).wait_recv()

    def drain(self):
        for k in range(1, self.n):
            other = lax.rem(self.me + k, self.n)
            self.copy(k, self.block(other), self.slot(self.me), self.target(other)).wait_send()


def rows_at(ref, size, index):
    return ref.at[pl.ds(pl.multiple_of(index * size, size), size)]


def dot(a, b):
    return jnp.dot(a, b, preferred_element_type=F32)


def dot_nt(a, b):
    return lax.dot_general(a, b, (((1,), (1,)), ((), ())), preferred_element_type=F32)


def dot_tn(a, b):
    return lax.dot_general(a, b, (((0,), (0,)), ((), ())), preferred_element_type=F32)


def iota(shape, axis):
    return lax.broadcasted_iota(jnp.int32, shape, axis)


def shuffle():
    new, old = iota((ROWS, ROWS), 0), iota((ROWS, ROWS), 1)
    source = ((new >> 2) & 7) * 16 + (new >> 5) * 4 + (new & 3)
    return (source == old).astype(F32).astype(BF16)


class Move:
    def __init__(self, out, source, first, middle, last, sems, slot):
        dp, y, zl, core, x = coords()
        t = zl * 2 + core
        self.out, self.source, self.first, self.middle, self.last = out, source, first, middle, last
        self.y, self.t = y, t
        near = lambda n, other: (dp, y * 8 + other, x)
        far = lambda n, other: (dp, other * 8 + t, x)
        send, recv = sems
        legs = ((8, t, near, 16), (4, y, far, 32))
        if not out:
            legs = legs[::-1]
        self.sizes = (legs[0][3], legs[1][3])
        self.mine = (legs[0][1], legs[1][1])
        self.legs = []
        for leg, (src, dst) in enumerate(((source, first), (middle, last))):
            n, me, target, size = legs[leg]
            self.legs.append(
                Exchange(
                    n,
                    me,
                    lambda other, target=target, n=n: target(n, other),
                    lambda other, src=src, size=size: rows_at(src, size, other),
                    lambda index, dst=dst, size=size: rows_at(dst, size, index),
                    send.at[slot, leg],
                    recv.at[slot, leg],
                )
            )

    def keep(self, leg, src, dst):
        size, me = self.sizes[leg], self.mine[leg]
        rows_at(dst, size, me)[...] = rows_at(src, size, me)[...]

    def start(self):
        self.legs[0].start()
        self.keep(0, self.source, self.first)

    def turn(self, order):
        self.legs[0].wait()
        if self.out:
            mixed = dot(order, self.first[...])
        else:
            mixed = dot_tn(order, self.first[...])
        self.middle[...] = mixed.astype(BF16)
        self.legs[1].start()
        self.keep(1, self.middle, self.last)

    def finish(self):
        self.legs[1].wait()

    def drain(self):
        self.legs[0].drain()
        self.legs[1].drain()


def inverse_of(values):
    return lax.rsqrt(jnp.sum(values * values, axis=-1, keepdims=True) * (1.0 / D) + EPSILON)


def norm_back(values, inverse, gain, grad):
    scaled = grad * gain
    cubed = inverse * inverse * inverse
    mean = jnp.sum(scaled * values, axis=-1, keepdims=True) * (1.0 / D)
    return inverse * scaled - values * (cubed * mean)


def span(h):
    low, high = h * HEAD_DIM, (h + 1) * HEAD_DIM
    begin, end = low // 128 * 128, -(-high // 128) * 128
    lane = iota((1, end - begin), 1) + begin
    keep = ((lane >= low) & (lane < high)).astype(F32).astype(BF16)
    return slice(begin, end), keep


def attend(q, k, v, bias, probs, out):
    out[...] = jnp.zeros_like(out)
    for h in range(HEADS):
        lanes, keep = span(h)
        scores = dot_nt(q[:, lanes] * keep, k[:, lanes]) * SCALE + bias
        raised = jnp.exp(scores - jnp.max(scores, axis=-1, keepdims=True))
        p = raised * (1.0 / jnp.sum(raised, axis=-1, keepdims=True))
        probs[h] = p
        out[:, lanes] += dot(p.astype(BF16), v[:, lanes] * keep)


def attend_back(q, k, v, probs, grad, dq, dk, dv):
    for ref in (dq, dk, dv):
        ref[...] = jnp.zeros_like(ref)
    for h in range(HEADS):
        lanes, keep = span(h)
        o = grad[:, lanes] * keep
        p = probs[h]
        dp = dot_nt(o, v[:, lanes])
        delta = jnp.sum(p * dp, axis=-1, keepdims=True)
        ds = (p * (dp - delta) * SCALE).astype(BF16)
        dq[:, lanes] += dot(ds, k[:, lanes] * keep)
        dk[:, lanes] += dot_tn(ds, q[:, lanes] * keep)
        dv[:, lanes] += dot_tn(p.astype(BF16), o)


def time_bias(time_mask):
    row, frame = iota((ROWS, 32), 0), iota((ROWS, 32), 1)
    spread = ((row >> 2) == frame).astype(F32).astype(BF16)
    mask = (time_mask[...] == 1).astype(F32).astype(BF16)
    mask = dot_nt(dot(spread, mask).astype(BF16), spread)
    a, b = iota((ROWS, ROWS), 0), iota((ROWS, ROWS), 1)
    fa, fb = a >> 2, b >> 2
    ok = ((a & 3) == (b & 3)) & ((fa == fb) | ((fb < fa) & (mask > 0.5)))
    return jnp.where(ok, 0.0, MASKED)


def space_bias(pattern, x):
    slot = iota((1, 256), 1) >> 6
    sides = []
    for row in range(2):
        bias = jnp.zeros((1, 256), F32)
        for r in range(4):
            block = 2 * x - 1 + r
            inside = (block >= 0) & (block < 8)
            seen = (pattern[row, r] == 1) | (r == row + 1)
            value = jnp.where(inside & seen, 0.0, MASKED)
            bias = jnp.where(slot == r, value, bias)
        sides.append(bias)
    return jnp.where(iota((ROWS, 256), 0) < 64, sides[0], sides[1])


def join_qkv(buf, whole):
    def body(i, carry):
        zh, x = i >> 1, (i & 1) * 2
        rows = pl.ds(pl.multiple_of(i * 144, 16), 144)
        pairs = (
            (buf[0, x, zh], buf[0, x + 1, zh], 0),
            (buf[1, zh, x], buf[1, zh, x + 1], 896),
        )
        for a, b, lane in pairs:
            pair = jnp.concatenate([a.reshape(72, 896), b.reshape(72, 896)], axis=0)
            whole[rows, lane : lane + 896] = pair
        return carry

    lax.fori_loop(0, 8, body, 0)


def join_out(buf, space, time):
    def body(zh, carry):
        rows = pl.ds(pl.multiple_of(zh * 144, 16), 144)
        for half in range(2):
            blocks = []
            for x in range(4):
                block = buf[0, x, zh] if half == 0 else buf[1, zh, x]
                blocks.append(block.astype(F32).reshape(72, 640))
            for ref, low in ((space, 0), (time, 36)):
                part = jnp.concatenate([block[low : low + 36] for block in blocks], axis=0)
                ref[rows, half * 640 : half * 640 + 640] = part.astype(BF16)
        return carry

    lax.fori_loop(0, 4, body, 0)


class Total:
    def __init__(self, gather, refs, sems, small):
        self.g = gather
        self.term, self.twin, self.r1, self.u, self.r2, self.v, self.rz, self.vz, self.rl, self.f = refs
        send, recv = sems
        self.small = small
        dp, y, zl, core, x = gather.pos
        term, u, r1, r2 = self.term, self.u, self.r1, self.r2
        self.e2 = Exchange(
            4, gather.p2, gather.along2, lambda i: term.at[core, i], lambda i: r1.at[i], send.at[0], recv.at[0]
        )
        self.e1 = Exchange(
            4, gather.p1, gather.along1, lambda i: u.at[i], lambda i: r2.at[i], send.at[1], recv.at[1]
        )
        self.el = Exchange(
            4,
            zl,
            lambda i: at(dp, y, i, core, x),
            lambda i: self.vz,
            lambda i: self.rl.at[i],
            send.at[2],
            recv.at[2],
        )

    def one(self, slot, src, dst, target, recv_slot=None):
        send, recv = self.small
        return pltpu.make_async_remote_copy(
            src_ref=src,
            dst_ref=dst,
            send_sem=send.at[slot],
            recv_sem=recv.at[slot if recv_slot is None else recv_slot],
            device_id=target,
            device_id_type=MESH,
        )

    def twin_id(self):
        dp, y, zl, core, x = self.g.pos
        return at(dp, y, zl, 1 - core, x)

    def start(self, att, up):
        dp, y, zl, core, x = self.g.pos
        for half in range(2):
            lanes = slice(0, 640) if half == 0 else slice(640, D)
            term = dot_tn(att[:, :WIDTH], up[:, lanes])
            if half == 1:
                term = jnp.concatenate([term, jnp.zeros((WIDTH, 128), F32)], axis=1)
            for s in range(16):
                block = jnp.concatenate([term[36 * s : 36 * s + 36], jnp.zeros((12, 640), F32)], axis=0)
                place = (0, s % 4, s // 4) if half == 0 else (1, s // 4, s % 4)
                self.term[place] = block.astype(BF16)
        self.one(0, self.term.at[1 - core], self.twin, self.twin_id()).start()

    def step1(self):
        dp, y, zl, core, x = self.g.pos
        self.one(0, self.twin, self.twin, self.twin_id()).wait_recv()
        for i in range(4):
            mine = self.term[core, i].astype(F32) + self.twin[i].astype(F32)
            self.term[core, i] = mine.astype(BF16)
        self.e2.start()

    def step2(self):
        dp, y, zl, core, x = self.g.pos
        self.e2.wait()
        p = self.g.p2
        total = self.term[core, p].astype(F32)
        for k in range(1, 4):
            total += self.r1[rem4(p + k)].astype(F32)
        self.u[...] = total.astype(BF16)
        self.e1.start()

    def step3(self):
        dp, y, zl, core, x = self.g.pos
        self.e1.wait()
        p = self.g.p1
        total = self.u[p].astype(F32)
        for k in range(1, 4):
            total += self.r2[rem4(p + k)].astype(F32)
        self.v[...] = total.astype(BF16)

        @pl.when(dp != y)
        def _():
            self.one(1, self.v, self.rz.at[dp], at(y, y, zl, core, x), 1 + rem4(dp - y)).start()

    def step4(self):
        dp, y, zl, core, x = self.g.pos

        @pl.when(dp == y)
        def _():
            total = self.v[...].astype(F32)
            for k in range(1, 4):
                source = rem4(dp + k)
                self.one(1, self.v, self.rz.at[source], self.twin_id(), 1 + k).wait_recv()
                total += self.rz[source].astype(F32)
            self.vz[...] = total.astype(BF16)
            self.el.start()

    def step5(self):
        dp, y, zl, core, x = self.g.pos

        @pl.when(dp == y)
        def _():
            self.el.wait()
            total = self.vz[...].astype(F32)
            for k in range(1, 4):
                total += self.rl[rem4(zl + k)].astype(F32)
            self.f[core] = total.astype(BF16)
            for k in range(1, 4):
                target = at(dp, rem4(y + k), zl, core, x)
                self.one(1 + k, self.f.at[core], self.f.at[core], target, 5).start()

        @pl.when(dp != y)
        def _():
            self.one(2, self.f.at[core], self.f.at[core], self.twin_id(), 5).wait_recv()

        self.one(5, self.f.at[core], self.f.at[core], self.twin_id(), 6).start()

    def step6(self, out):
        dp, y, zl, core, x = self.g.pos
        self.one(5, self.f.at[1 - core], self.f.at[1 - core], self.twin_id(), 6).wait_recv()
        out[:, :640] = self.f[0][:36].astype(F32)
        out[:, 640:] = self.f[1][:36, :512].astype(F32)

    def drain(self):
        dp, y, zl, core, x = self.g.pos
        self.one(0, self.term.at[1 - core], self.twin, self.twin_id()).wait_send()
        self.e2.drain()
        self.e1.drain()

        @pl.when(dp != y)
        def _():
            self.one(1, self.v, self.rz.at[dp], self.twin_id()).wait_send()

        @pl.when(dp == y)
        def _():
            self.el.drain()
            for k in range(1, 4):
                self.one(1 + k, self.f.at[core], self.f.at[core], self.twin_id()).wait_send()

        self.one(5, self.f.at[core], self.f.at[core], self.twin_id()).wait_send()


def halo_copies(low, high, from_low, from_high, sems, slot):
    dp, y, zl, core, x = coords()
    send, recv = sems
    return [
        pltpu.make_async_remote_copy(
            src_ref=src,
            dst_ref=dst,
            send_sem=send.at[slot, i],
            recv_sem=recv.at[slot, i],
            device_id=at(dp, y, zl, core, rem4(x + step)),
            device_id_type=MESH,
        )
        for i, (src, dst, step) in enumerate(((low, from_high, -1), (high, from_low, 1)))
    ]


def kernel(
    latents,
    upstream,
    modulation,
    space_qkv,
    space_out,
    time_qkv,
    time_out,
    pattern,
    time_mask,
    result,
    start_grad,
    out_grad,
    s,
):
    dp, y, zl, core, x = coords()
    gather = Gather((s["g0"], s["g1"], s["g2"]), s["g_send"], s["g_recv"])
    sems = (s["m_send"], s["m_recv"])
    halo_sems = (s["h_send"], s["h_recv"])

    def move(out, name, source, slot):
        return Move(out, source, s[name + "1"], s[name + "2"], s[name + "3"], sems, slot)

    lat_move = move(True, "lat", latents, 0)
    up_move = move(True, "up", upstream, 1)
    att_move = move(True, "att", s["att"], 2)
    back_att = move(False, "batt", s["tatt"], 3)
    back_grad = move(False, "bgrad", s["sgrad"], 4)
    back_mid = move(False, "bmid", s["mid_grad"], 5)
    total = Total(
        gather,
        [s[n] for n in ("term", "twin", "r1", "u", "r2", "v", "rz", "vz", "rl", "f")],
        (s["t_send"], s["t_recv"]),
        (s["o_send"], s["o_recv"]),
    )

    place_own(gather, space_qkv, space_out, time_qkv, time_out)
    greet()
    for g in range(3):
        gather.zsend(g)

    start = latents[...].astype(F32)
    gain_space = 1.0 + modulation[0:1, :]
    gain_time = 1.0 + modulation[1:2, :]
    inverse = inverse_of(start)
    s["inv_s"][...] = inverse
    s["normed"][...] = (start * inverse * gain_space).astype(BF16)
    order = shuffle()
    s["order"][...] = order

    gather.zpass(0)
    gather.s1send(0)
    gather.zpass(1)
    gather.s1pass(0)
    gather.s2send(0)
    gather.zpass(2)
    lat_move.start()
    up_move.start()
    gather.s1send(1)
    gather.s1pass(1)
    gather.s2pass(0)
    gather.s2send(1)
    gather.s1send(2)
    gather.s2done(0)
    gather.s1pass(2)
    gather.end(0)

    join_qkv(s["g0"], s["w0"])
    rows = dot(s["normed"][...], s["w0"][...])
    s["q"][...] = rows[:, :WIDE].astype(BF16)
    s["kv"][0, 64:192] = rows[:, WIDTH : WIDTH + WIDE].astype(BF16)
    s["kv"][1, 64:192] = rows[:, 2 * WIDTH : 2 * WIDTH + WIDE].astype(BF16)
    kv = s["kv"]
    halo = halo_copies(
        kv.at[:, pl.ds(64, 64)],
        kv.at[:, pl.ds(128, 64)],
        kv.at[:, pl.ds(0, 64)],
        kv.at[:, pl.ds(192, 64)],
        halo_sems,
        0,
    )
    for copy in halo:
        copy.start()
    gather.s2pass(1)
    gather.s2send(2)
    lat_move.turn(s["order"][...])
    up_move.turn(s["order"][...])
    bias = space_bias(pattern, x)
    for copy in halo:
        copy.wait_recv()
    attend(s["q"], kv.at[0], kv.at[1], bias, s["probs_s"], s["acc"])
    s["att"][...] = s["acc"][...].astype(BF16)
    att_move.start()
    gather.s2done(1)
    gather.end(1)
    join_out(s["g1"], s["so"], s["to"])
    s["mid_f"][...] = latents[...].astype(F32) + dot(s["att"][:, :WIDTH], s["so"][:, :D])
    att_move.turn(s["order"][...])
    gather.s2pass(2)
    up_move.finish()
    lat_move.finish()
    s["tgrad"][:, :WIDTH] = dot_nt(s["up3"][...], s["to"][:, :D]).astype(BF16)
    s["tgrad"][:, WIDTH:] = jnp.zeros((ROWS, WIDE - WIDTH), BF16)
    s["tbias"][...] = time_bias(time_mask)
    gather.s2done(2)
    gather.end(2)
    join_qkv(s["g2"], s["w2"])
    att_move.finish()

    middle = s["lat3"][...].astype(F32) + dot(s["att3"][:, :WIDTH], s["so"][:, :D])
    inverse = inverse_of(middle)
    s["inv_t"][...] = inverse
    s["mid_p"][...] = middle
    rows = dot((middle * inverse * gain_time).astype(BF16), s["w2"][...])
    s["tq"][...] = rows[:, :WIDE].astype(BF16)
    s["tk"][...] = rows[:, WIDTH : WIDTH + WIDE].astype(BF16)
    s["tv"][...] = rows[:, 2 * WIDTH : 2 * WIDTH + WIDE].astype(BF16)
    attend(s["tq"], s["tk"], s["tv"], s["tbias"][...], s["probs_t"], s["acc"])
    s["tatt"][...] = s["acc"][...].astype(BF16)
    back_att.start()
    total.start(s["tatt"], s["up3"])

    attend_back(s["tq"], s["tk"], s["tv"], s["probs_t"], s["tgrad"], s["acc"], s["tdk"], s["tdv"])
    s["grads"][:, :WIDTH] = s["acc"][:, :WIDTH].astype(BF16)
    s["grads"][:, WIDTH : 2 * WIDTH] = s["tdk"][:, :WIDTH].astype(BF16)
    s["grads"][:, 2 * WIDTH :] = s["tdv"][...].astype(BF16)
    grad = dot_nt(s["grads"][...], s["w2"][...])
    mid_grad = s["up3"][...].astype(F32) + norm_back(s["mid_p"][...], s["inv_t"][...], gain_time, grad)
    s["mid_grad"][...] = mid_grad.astype(BF16)
    s["sgrad"][:, :WIDTH] = dot_nt(s["mid_grad"][...], s["so"][:, :D]).astype(BF16)
    s["sgrad"][:, WIDTH:] = jnp.zeros((ROWS, WIDE - WIDTH), BF16)
    back_grad.start()
    back_mid.start()
    back_att.turn(s["order"][...])
    total.step1()
    back_grad.turn(s["order"][...])
    back_mid.turn(s["order"][...])
    back_att.finish()
    result[...] = (s["mid_f"][...] + dot(s["batt3"][:, :WIDTH], s["to"][:, :D])).astype(BF16)
    total.step2()
    back_grad.finish()

    attend_back(s["q"], kv.at[0], kv.at[1], s["probs_s"], s["bgrad3"], s["acc"], s["dkv"].at[0], s["dkv"].at[1])
    s["rim"][0] = s["dkv"][:, :64].astype(BF16)
    s["rim"][1] = s["dkv"][:, 192:].astype(BF16)
    rim = halo_copies(
        s["rim"].at[0], s["rim"].at[1], s["rim_in"].at[0], s["rim_in"].at[1], halo_sems, 1
    )
    for copy in rim:
        copy.start()
    total.step3()
    grad = dot_nt(s["acc"][...].astype(BF16), s["w0"][:, :WIDE])
    total.step4()
    for copy in rim:
        copy.wait_recv()
    own = s["dkv"][:, 64:192]
    edges = jnp.concatenate([s["rim_in"][0], s["rim_in"][1]], axis=1).astype(F32)
    own = (own + edges).astype(BF16)
    s["grads"][:, WIDTH : 2 * WIDTH] = own[0][:, :WIDTH]
    s["grads"][:, 2 * WIDTH :] = own[1]
    s["grads"][:, 512:WIDTH] = jnp.zeros((ROWS, 64), BF16)
    grad += dot_nt(s["grads"][:, 512:], s["w0"][:, 512:])
    back_mid.finish()
    start = latents[...].astype(F32)
    back = norm_back(start, s["inv_s"][...], gain_space, grad)
    start_grad[...] = (s["bmid3"][...].astype(F32) + back).astype(BF16)
    total.step5()
    total.step6(out_grad)

    for g in range(3):
        gather.drain(g)
    for each in (lat_move, up_move, att_move, back_att, back_grad, back_mid, total):
        each.drain()
    for copy in halo + rim:
        copy.wait_send()


def scratch():
    def vmem(shape, dtype=BF16):
        return pltpu.VMEM(shape, dtype)

    dma = pltpu.SemaphoreType.DMA
    out = {f"g{g}": vmem((2, 4, 4, 9, 8, lanes)) for g, lanes in enumerate(LANES)}
    out.update(g_send=dma((3, 16)), g_recv=dma((3, 16)), m_send=dma((6, 2, 7)), m_recv=dma((6, 2, 7)))
    out.update(h_send=dma((2, 2)), h_recv=dma((2, 2)), t_send=dma((3, 3)), t_recv=dma((3, 3)))
    out.update(o_send=dma((8,)), o_recv=dma((8,)))
    out.update(w0=vmem((D, 1792)), w2=vmem((D, 1792)), so=vmem((WIDTH, 1280)), to=vmem((WIDTH, 1280)))
    for name, lanes in (("lat", D), ("up", D), ("att", WIDE), ("batt", WIDE), ("bgrad", WIDE), ("bmid", D)):
        for leg in range(1, 4):
            out[f"{name}{leg}"] = vmem((ROWS, lanes))
    for name in ("att", "tatt", "sgrad", "q", "tq", "tk", "tv", "tgrad"):
        out[name] = vmem((ROWS, WIDE))
    out.update(normed=vmem((ROWS, D)), mid_grad=vmem((ROWS, D)), order=vmem((ROWS, ROWS)))
    out.update(kv=vmem((2, 256, WIDE)), grads=vmem((ROWS, 1792)))
    out.update(rim=vmem((2, 2, 64, WIDE)), rim_in=vmem((2, 2, 64, WIDE)))
    out.update(inv_s=vmem((ROWS, 1), F32), inv_t=vmem((ROWS, 1), F32), tbias=vmem((ROWS, ROWS), F32))
    out.update(acc=vmem((ROWS, WIDE), F32), tdk=vmem((ROWS, WIDE), F32), tdv=vmem((ROWS, WIDE), F32))
    out.update(dkv=vmem((2, 256, WIDE), F32), mid_f=vmem((ROWS, D), F32), mid_p=vmem((ROWS, D), F32))
    out.update(probs_s=vmem((HEADS, ROWS, 256), F32), probs_t=vmem((HEADS, ROWS, ROWS), F32))
    block = (48, WIDE)
    out.update(term=vmem((2, 4, 4) + block), twin=vmem((4, 4) + block), r1=vmem((4, 4) + block))
    out.update(u=vmem((4,) + block), r2=vmem((4,) + block), v=vmem(block), rz=vmem((4,) + block))
    out.update(vz=vmem(block), rl=vmem((4,) + block), f=vmem((2,) + block))
    return out


def local(
    latents,
    upstream,
    modulation,
    space_qkv,
    space_out,
    time_qkv,
    time_out,
    space_pattern,
    time_mask,
):
    shapes = scratch()
    names = list(shapes)

    def body(*refs):
        kernel(*refs[:12], dict(zip(names, refs[12:])))

    vmem = pl.BlockSpec(memory_space=pltpu.VMEM)
    smem = pl.BlockSpec(memory_space=pltpu.SMEM)
    result, start_grad, out_grad = pl.pallas_call(
        body,
        out_shape=[
            jax.ShapeDtypeStruct((ROWS, D), BF16),
            jax.ShapeDtypeStruct((ROWS, D), BF16),
            jax.ShapeDtypeStruct((36, D), F32),
        ],
        in_specs=[vmem] * 7 + [smem, vmem],
        out_specs=[vmem] * 3,
        scratch_shapes=list(shapes.values()),
        compiler_params=pltpu.CompilerParams(
            collective_id=0, has_side_effects=True, vmem_limit_bytes=60 << 20
        ),
    )(
        latents.reshape(ROWS, D),
        upstream.reshape(ROWS, D),
        modulation.reshape(2, D),
        space_qkv,
        space_out,
        time_qkv,
        time_out,
        space_pattern,
        time_mask,
    )
    return (result.reshape(latents.shape), start_grad.reshape(latents.shape), out_grad)


def solution(mesh):
    in_specs = (
        P("dp", "seq", "tile", None),
        P("dp", "seq", "tile", None),
        P("dp", None, None),
        P(("dp", "tile"), None),
        P(("dp", "tile"), None),
        P(("dp", "tile"), None),
        P(("dp", "tile"), None),
        P("tile", None),
        P(),
    )
    out_specs = (
        P("dp", "seq", "tile", None),
        P("dp", "seq", "tile", None),
        P(("dp", "tile"), None),
    )
    return jax.shard_map(local, mesh=mesh, in_specs=in_specs, out_specs=out_specs, check_vma=False)
```

time: 701 us -> 139 us (0.20)
  the two profiles are of different devices: /device:TPU:1 before, /device:TPU:19 now
where the time goes in v2:
time: 139 us
  Pallas kernels  134 us (96%)
  local copies, waits for them, and re-layouts  3.45 us (2%)
    pallas_call x1, Pallas kernels, local(): pl.pallas_call(body, out_shape=[jax.ShapeDtypeStruct((ROWS, D), BF16), ja...  134 us
    unnamed x7, local copies, waits for them, and re-layouts  3.45 us

profile of v2, /device:TPU:19, one launch (start us, length us, event | category | flops | bytes accessed | tf_op | source)
XLA Modules:
  0.0 138.5 jit_solution(18147715591839682293)
XLA Ops:
  0.6 134.4 %shard_map.112 = (bf16[128,1152]{1,0:T(8,128)(2,1)}, bf16[128,1152]{1,0:T(8,128)(2,1)}, f32[36,1152]{1,0:T(8,128)}) custom-call(bf16[128,1152]{1,0:T(8,128)(2,1)} %bitcast.5, bf16[128,1152]{1,0:T(8,128)(2,1)} %bitcast.6, f32[2,1152]{1,0:T(2,128)} %bitcast.9, bf16[72,1728]{1,0:T(8,128)(2,1)} %refs_3_.1, bf16[36,1152]{1,0:T(8,128)(2,1)} %refs_4_.1, ...), custom_call_target="tpu_custom_call" | custom-call | tf_op jit(solution)/shard_map/pallas_call | solution.py:808
  135.1 0.0 copy-start
  135.1 1.7 %copy.15 = bf16[1,1,128,1152]{3,2,1,0:T(8,128)(2,1)} copy(bf16[1,1,128,1152]{3,2,1,0:T(8,128)(2,1)} %bitcast.8) | data formatting | bytes 589824
  136.8 0.0 copy-done
  136.8 0.0 copy-start.1
  136.8 0.7 copy.16
  137.5 0.3 copy-done.1
  137.8 0.7 copy.17
Async XLA Ops:
  135.1 1.8 %copy-start = (bf16[128,1152]{1,0:T(8,128)(2,1)S(1)}, bf16[128,1152]{1,0:T(8,128)(2,1)}, u32[]{:S(2)}) copy-start(bf16[128,1152]{1,0:T(8,128)(2,1)} %get-tuple-element.7) | copy-start | bytes 884740
  136.8 1.0 copy-start.1

commit v3 on v2

v3 whole, which is shorter than its diff:
```python
import jax
import jax.numpy as jnp
from jax import lax
from jax.experimental import pallas as pl
from jax.experimental.pallas import tpu as pltpu
from jax.sharding import PartitionSpec as P

HEADS = 8
HEAD_DIM = 72
WIDTH = HEADS * HEAD_DIM
WIDE = 640
D = 1152
ROWS = 128
EPSILON = 1e-06
MASKED = -1e30
SCALE = HEAD_DIM ** (-0.5)
BF16 = jnp.bfloat16
F32 = jnp.float32

MESH = pl.DeviceIdType.MESH
LANES = (896, 640, 896)


def coords():
    dp, seq, tile = lax.axis_index("dp"), lax.axis_index("seq"), lax.axis_index("tile")
    return dp, seq // 8, (seq // 2) % 4, seq % 2, tile


def at(dp, y, zl, core, tile):
    return (dp, (y * 4 + zl) * 2 + core, tile)


def rem4(value):
    return lax.rem(value + 8, 4)


class Gather:
    def __init__(self, bufs, send, recv):
        self.bufs, self.send, self.recv = bufs, send, recv
        dp, y, zl, core, x = self.pos = coords()
        self.first = core == 0
        self.p1 = jnp.where(self.first, y, x)
        self.p2 = jnp.where(self.first, x, y)
        self.q1 = jnp.where(self.first, x, y)
        self.q2 = jnp.where(self.first, y, x)

    def along1(self, place):
        dp, y, zl, core, x = self.pos
        place = rem4(place)
        return at(dp, jnp.where(self.first, place, y), zl, core, jnp.where(self.first, x, place))

    def along2(self, place):
        dp, y, zl, core, x = self.pos
        place = rem4(place)
        return at(dp, jnp.where(self.first, y, place), zl, core, jnp.where(self.first, place, x))

    def copy(self, g, ref, slot, target=None, recv_slot=None):
        return pltpu.make_async_remote_copy(
            src_ref=ref,
            dst_ref=ref,
            send_sem=self.send.at[g, slot],
            recv_sem=self.recv.at[g, slot if recv_slot is None else recv_slot],
            device_id=at(*self.pos) if target is None else target,
            device_id_type=MESH,
        )

    def block(self, g, i2, i1):
        return self.bufs[g].at[self.pos[3], rem4(i2), rem4(i1)]

    def own(self, g):
        return self.block(g, self.p2, self.p1)

    def third(self, g, t):
        return self.own(g).at[pl.ds(3 * t, 3)]

    def source(self, t):
        return rem4(self.pos[1] - t)

    def zsend(self, g):
        dp, y, zl, core, x = self.pos

        @pl.when((zl < 3) & (dp == self.source(zl)))
        def _():
            for k in range(1, 4):
                self.copy(g, self.third(g, zl), k - 1, at(rem4(dp + k), y, zl, core, x), 0).start()

    def neighbours(self):
        dp, y, zl, core, x = self.pos
        z = dp * 4 + zl
        for i, step in enumerate((1, -1, jnp.where(zl == 2, -2, 2))):
            other = lax.rem(z + step + 16, 16)
            yield i, other // 4, at(other // 4, y, lax.rem(other, 4), core, x)

    def zpass(self, g):
        dp, y, zl, core, x = self.pos

        @pl.when((zl < 3) & (dp != self.source(zl)))
        def _():
            self.copy(g, self.third(g, zl), 0, None, 0).wait_recv()

        for i, their, target in self.neighbours():

            @pl.when((zl < 3) & (their != self.source(zl)))
            def _():
                self.copy(g, self.third(g, zl), 16 + i, target, 1 + zl).start()

    def zdone(self, g):
        dp, y, zl, core, x = self.pos
        for t in range(3):

            @pl.when((dp != self.source(t)) & (zl != t))
            def _():
                self.copy(g, self.third(g, t), 0, None, 1 + t).wait_recv()

    def zend(self, g):
        dp, y, zl, core, x = self.pos

        @pl.when((zl < 3) & (dp == self.source(zl)))
        def _():
            for k in range(3):
                self.copy(g, self.third(g, zl), k).wait_send()

        for i, their, target in self.neighbours():

            @pl.when((zl < 3) & (their != self.source(zl)))
            def _():
                self.copy(g, self.third(g, zl), 16 + i).wait_send()

    def ring(self, g, axis, j, k):
        base = 4 if axis == 1 else 20 + 4 * j
        along, p = (self.along1, self.p1) if axis == 1 else (self.along2, self.p2)
        return base, along, p

    def push(self, g, axis, j=0):
        base, along, p = self.ring(g, axis, j, 0)
        ref = self.block(g, self.p2, self.p1 - j)
        self.copy(g, ref, base, along(p + 1)).start()
        self.copy(g, ref, base + 1, along(p - 1)).start()

    def seen(self, g, axis, j, k):
        return self.block(g, self.p2, self.p1 - k) if axis == 1 else self.block(g, self.p2 - k, self.p1 - j)

    def onward(self, g, axis, j, k):
        base, along, p = self.ring(g, axis, j, k)
        ref = self.seen(g, axis, j, k)
        if k == 1:
            self.copy(g, ref, base).wait_recv()
            self.copy(g, ref.at[pl.ds(0, 5)], base + 2, along(p + 1)).start()
        else:
            self.copy(g, ref, base + 1).wait_recv()
            self.copy(g, ref.at[pl.ds(5, 4)], base + 3, along(p - 1)).start()

    def last(self, g, axis, j):
        base, along, p = self.ring(g, axis, j, 2)
        ref = self.seen(g, axis, j, 2)
        self.copy(g, ref.at[pl.ds(0, 5)], base + 2).wait_recv()
        self.copy(g, ref.at[pl.ds(5, 4)], base + 3).wait_recv()

    def sent(self, g, axis, j):
        base, along, p = self.ring(g, axis, j, 0)
        self.copy(g, self.own(g), base).wait_send()
        self.copy(g, self.own(g), base + 1).wait_send()
        self.copy(g, self.own(g).at[pl.ds(0, 5)], base + 2).wait_send()
        self.copy(g, self.own(g).at[pl.ds(5, 4)], base + 3).wait_send()

    def twin(self, g, k, j):
        dp, y, zl, core, x = self.pos
        ref = self.block(g, self.p2 - k, self.p1 - j)
        self.copy(g, ref, 40 + 4 * j + k, at(dp, y, zl, 1 - core, x)).start()

    def round(self, g, j):
        self.push(g, 2, j)
        self.twin(g, 0, j)

    def open(self, g):
        self.zdone(g)
        self.push(g, 1)
        self.round(g, 0)

    def s1mid(self, g):
        for k in (1, 3):
            self.onward(g, 1, 0, k)
            self.round(g, k)

    def s1end(self, g):
        self.last(g, 1, 0)
        self.round(g, 2)

    def mid(self, g, *rounds):
        for j in rounds:
            for k in (1, 3):
                self.onward(g, 2, j, k)
                self.twin(g, k, j)

    def fin(self, g, *rounds):
        for j in rounds:
            self.last(g, 2, j)
            self.twin(g, 2, j)

    def end(self, g):
        for j in (0, 1, 3, 2):
            for k in (0, 1, 3, 2):
                ref = self.bufs[g].at[1 - self.pos[3], rem4(self.q2 - k), rem4(self.q1 - j)]
                self.copy(g, ref, 40 + 4 * j + k).wait_recv()

    def drain(self, g):
        self.zend(g)
        self.sent(g, 1, 0)
        for j in range(4):
            self.sent(g, 2, j)
            for k in range(4):
                self.copy(g, self.own(g), 40 + 4 * j + k).wait_send()


def greet():
    dp, y, zl, core, x = coords()
    seq = lax.axis_index("seq")
    barrier = pltpu.get_barrier_semaphore()

    def hello(target):
        pl.semaphore_signal(barrier, inc=1, device_id=target, device_id_type=MESH)

    def frame(k, carry):
        hello((dp, lax.rem(seq + k, 32), x))
        return carry

    lax.fori_loop(1, 32, frame, 0)
    for k in range(1, 4):
        hello(at(rem4(dp + k), y, zl, core, x))
        hello(at(dp, y, zl, core, rem4(x + k)))
    for step in (1, 3):
        hello(at(rem4(dp + step), y, 3 - zl, core, x))
    pl.semaphore_wait(barrier, 39)


def place_own(gather, space_qkv, space_out, time_qkv, time_out):
    dp, y, zl, core, x = gather.pos

    def put(g, block):
        block = block.reshape(9, 8, LANES[g])
        for t in range(3):

            @pl.when(dp == gather.source(t))
            def _():
                gather.third(g, t)[...] = block[3 * t : 3 * t + 3]

    for half in range(2):

        @pl.when(core == half)
        def _():
            for g, ref in ((0, space_qkv), (2, time_qkv)):
                if half == 0:
                    block = ref[:, :896]
                else:
                    block = jnp.concatenate([ref[:, 896:], jnp.zeros((72, 64), BF16)], axis=1)
                put(g, block)
            block = jnp.concatenate([space_out[...].astype(F32), time_out[...].astype(F32)], axis=0)
            if half == 0:
                block = block[:, :640]
            else:
                block = jnp.concatenate([block[:, 640:], jnp.zeros((72, 128), F32)], axis=1)
            put(1, block.astype(BF16))


class Exchange:
    def __init__(self, n, me, target, block, slot, send, recv):
        self.n, self.me, self.target = n, me, target
        self.block, self.slot, self.sems = block, slot, (send, recv)

    def copy(self, k, src, dst, target):
        return pltpu.make_async_remote_copy(
            src_ref=src,
            dst_ref=dst,
            send_sem=self.sems[0].at[k - 1],
            recv_sem=self.sems[1].at[k - 1],
            device_id=target,
            device_id_type=MESH,
        )

    def start(self):
        for k in range(1, self.n):
            other = lax.rem(self.me + k, self.n)
            self.copy(k, self.block(other), self.slot(self.me), self.target(other)).start()

    def wait(self):
        for k in range(1, self.n):
            source = lax.rem(self.me + self.n - k, self.n)
            self.copy(k, self.slot(source), self.slot(source), self.target(source)).wait_recv()

    def drain(self):
        for k in range(1, self.n):
            other = lax.rem(self.me + k, self.n)
            self.copy(k, self.block(other), self.slot(self.me), self.target(other)).wait_send()


def dot(a, b):
    return jnp.dot(a, b, preferred_element_type=F32)


def dot_nt(a, b):
    return lax.dot_general(a, b, (((1,), (1,)), ((), ())), preferred_element_type=F32)


def dot_tn(a, b):
    return lax.dot_general(a, b, (((0,), (0,)), ((), ())), preferred_element_type=F32)


def iota(shape, axis):
    return lax.broadcasted_iota(jnp.int32, shape, axis)


class Move:
    def __init__(self, out, source, target, sems, slot):
        self.out, self.source, self.target, self.sems, self.slot = out, source, target, sems, slot
        self.tile, self.dp, self.seq = lax.axis_index("tile"), lax.axis_index("dp"), lax.axis_index("seq")

    def patches(self, seq):
        return (seq & 7) * 4 + (seq >> 3)

    def src(self, other):
        return self.source.at[self.patches(other) if self.out else other]

    def dst(self, owner):
        return self.target.at[owner if self.out else self.patches(owner)]

    def copy(self, k, other, owner):
        send, recv = self.sems
        return pltpu.make_async_remote_copy(
            src_ref=self.src(other),
            dst_ref=self.dst(owner),
            send_sem=send.at[self.slot, k],
            recv_sem=recv.at[self.slot, k],
            device_id=(self.dp, other, self.tile),
            device_id_type=MESH,
        )

    def each(self, step):
        def body(k, carry):
            step(k)
            return carry

        lax.fori_loop(1, 32, body, 0)

    def start(self):
        self.each(lambda k: self.copy(k, lax.rem(self.seq + k, 32), self.seq).start())
        self.dst(self.seq)[...] = self.src(self.seq)[...]

    def finish(self):
        self.each(lambda k: self.copy(k, self.seq, lax.rem(self.seq + 32 - k, 32)).wait_recv())

    def drain(self):
        self.each(lambda k: self.copy(k, self.seq, self.seq).wait_send())


def inverse_of(values):
    return lax.rsqrt(jnp.sum(values * values, axis=-1, keepdims=True) * (1.0 / D) + EPSILON)


def norm_back(values, inverse, gain, grad):
    scaled = grad * gain
    cubed = inverse * inverse * inverse
    mean = jnp.sum(scaled * values, axis=-1, keepdims=True) * (1.0 / D)
    return inverse * scaled - values * (cubed * mean)


def span(h):
    low, high = h * HEAD_DIM, (h + 1) * HEAD_DIM
    begin, end = low // 128 * 128, -(-high // 128) * 128
    lane = iota((1, end - begin), 1) + begin
    keep = ((lane >= low) & (lane < high)).astype(F32).astype(BF16)
    return slice(begin, end), keep


def attend(q, k, v, bias, probs, out):
    out[...] = jnp.zeros_like(out)
    for h in range(HEADS):
        lanes, keep = span(h)
        scores = dot_nt(q[:, lanes] * keep, k[:, lanes]) * SCALE + bias
        raised = jnp.exp(scores - jnp.max(scores, axis=-1, keepdims=True))
        p = raised * (1.0 / jnp.sum(raised, axis=-1, keepdims=True))
        probs[h] = p
        out[:, lanes] += dot(p.astype(BF16), v[:, lanes] * keep)


def attend_back(q, k, v, probs, grad, dq, dk, dv):
    for ref in (dq, dk, dv):
        ref[...] = jnp.zeros_like(ref)
    for h in range(HEADS):
        lanes, keep = span(h)
        o = grad[:, lanes] * keep
        p = probs[h]
        dp = dot_nt(o, v[:, lanes])
        delta = jnp.sum(p * dp, axis=-1, keepdims=True)
        ds = (p * (dp - delta) * SCALE).astype(BF16)
        dq[:, lanes] += dot(ds, k[:, lanes] * keep)
        dk[:, lanes] += dot_tn(ds, q[:, lanes] * keep)
        dv[:, lanes] += dot_tn(p.astype(BF16), o)


def space_back_rim(q, v, probs, grad, ds_all, rim):
    rim[...] = jnp.zeros_like(rim)
    for h in range(HEADS):
        lanes, keep = span(h)
        o = grad[:, lanes] * keep
        p = probs[h]
        dp = dot_nt(o, v[:, lanes])
        delta = jnp.sum(p * dp, axis=-1, keepdims=True)
        ds = (p * (dp - delta) * SCALE).astype(BF16)
        ds_all[h] = ds
        rim[0, :, lanes] += dot_tn(ds[:, 128:], q[:, lanes] * keep)
        rim[1, :, lanes] += dot_tn(p[:, 128:].astype(BF16), o)


def space_back_own(q, k, probs, grad, ds_all, dq, dkv):
    dq[...] = jnp.zeros_like(dq)
    dkv[...] = jnp.zeros_like(dkv)
    for h in range(HEADS):
        lanes, keep = span(h)
        ds = ds_all[h]
        dq[:, lanes] += dot(ds, k[:, lanes] * keep)
        dkv[0, :, lanes] += dot_tn(ds[:, :128], q[:, lanes] * keep)
        dkv[1, :, lanes] += dot_tn(probs[h, :, :128].astype(BF16), grad[:, lanes] * keep)


def time_bias(time_mask):
    row, frame = iota((ROWS, 32), 0), iota((ROWS, 32), 1)
    spread = ((row >> 2) == frame).astype(F32).astype(BF16)
    mask = (time_mask[...] == 1).astype(F32).astype(BF16)
    mask = dot_nt(dot(spread, mask).astype(BF16), spread)
    a, b = iota((ROWS, ROWS), 0), iota((ROWS, ROWS), 1)
    fa, fb = a >> 2, b >> 2
    ok = ((a & 3) == (b & 3)) & ((fa == fb) | ((fb < fa) & (mask > 0.5)))
    return jnp.where(ok, 0.0, MASKED)


def space_bias(pattern, x):
    part = iota((1, 256), 1) >> 6
    slot = jnp.where(part < 2, part + 1, jnp.where(part == 2, 0, 3))
    sides = []
    for row in range(2):
        bias = jnp.zeros((1, 256), F32)
        for r in range(4):
            block = 2 * x - 1 + r
            inside = (block >= 0) & (block < 8)
            seen = (pattern[row, r] == 1) | (r == row + 1)
            value = jnp.where(inside & seen, 0.0, MASKED)
            bias = jnp.where(slot == r, value, bias)
        sides.append(bias)
    return jnp.where(iota((ROWS, 256), 0) < 64, sides[0], sides[1])


def shard(buf, half, zh, x):
    first = half == 0
    parts = []
    for t in range(3):
        share = rem4(zh + t)
        part = buf[half, jnp.where(first, x, share), jnp.where(first, share, x)]
        parts.append(part[3 * t : 3 * t + 3])
    return jnp.concatenate(parts, axis=0).reshape(72, buf.shape[-1])


def join_qkv(buf, whole, half):
    lanes = pl.ds(pl.multiple_of(half * 896, 128), 896)

    def body(i, carry):
        zh, x = i >> 1, (i & 1) * 2
        rows = pl.ds(pl.multiple_of(i * 144, 16), 144)
        pair = jnp.concatenate([shard(buf, half, zh, x), shard(buf, half, zh, x + 1)], axis=0)
        whole[rows, lanes] = pair
        return carry

    lax.fori_loop(0, 8, body, 0)


def join_out(buf, space, time, half):
    lanes = pl.ds(pl.multiple_of(half * 640, 128), 640)

    def body(zh, carry):
        rows = pl.ds(pl.multiple_of(zh * 144, 16), 144)
        blocks = [shard(buf, half, zh, x).astype(F32) for x in range(4)]
        for ref, low in ((space, 0), (time, 36)):
            part = jnp.concatenate([block[low : low + 36] for block in blocks], axis=0)
            ref[rows, lanes] = part.astype(BF16)
        return carry

    lax.fori_loop(0, 4, body, 0)


class Total:
    def __init__(self, gather, refs, sems, small):
        self.g = gather
        self.term, self.r1, self.u, self.r2, self.v, self.ra, self.va, self.rb, self.f = refs
        send, recv = sems
        self.small = small
        dp, y, zl, core, x = gather.pos
        term, u, r1, r2 = self.term, self.u, self.r1, self.r2
        self.e2 = Exchange(
            4, gather.p2, gather.along2, lambda i: term.at[i], lambda i: r1.at[i], send.at[0], recv.at[0]
        )
        self.e1 = Exchange(
            4, gather.p1, gather.along1, lambda i: u.at[i], lambda i: r2.at[i], send.at[1], recv.at[1]
        )

    def one(self, slot, src, dst, target, recv_slot=None):
        send, recv = self.small
        return pltpu.make_async_remote_copy(
            src_ref=src,
            dst_ref=dst,
            send_sem=send.at[slot],
            recv_sem=recv.at[slot if recv_slot is None else recv_slot],
            device_id=target,
            device_id_type=MESH,
        )

    def twin_id(self):
        dp, y, zl, core, x = self.g.pos
        return at(dp, y, zl, 1 - core, x)

    def share(self, up, up2):
        self.one(0, up, up2, self.twin_id()).start()

    def give(self, att, att2):
        self.one(12, att, att2, self.twin_id(), 14).start()

    def step1(self, att, att2, up, up_in, up2):
        dp, y, zl, core, x = self.g.pos
        self.one(0, up_in, up2, self.twin_id()).wait_recv()
        self.one(12, att, att2, self.twin_id(), 14).wait_recv()
        for half in range(2):

            @pl.when(core == half)
            def _():
                lanes = slice(0, 640) if half == 0 else slice(640, D)
                term = dot_tn(att[:, :WIDTH], up[:, lanes])
                term += dot_tn(att2[:, :WIDTH], up2[:, :, lanes].reshape(ROWS, -1))
                if half == 1:
                    term = jnp.concatenate([term, jnp.zeros((WIDTH, 128), F32)], axis=1)
                for i in range(16):
                    block = jnp.concatenate([term[36 * i : 36 * i + 36], jnp.zeros((12, 640), F32)], axis=0)
                    place = (i % 4, i // 4) if half == 0 else (i // 4, i % 4)
                    self.term[place] = block.astype(BF16)

        self.e2.start()

    def step2(self):
        dp, y, zl, core, x = self.g.pos
        self.e2.wait()
        p = self.g.p2
        total = self.term[p].astype(F32)
        for k in range(1, 4):
            total += self.r1[rem4(p + k)].astype(F32)
        self.u[...] = total.astype(BF16)
        self.e1.start()

    def step3(self):
        dp, y, zl, core, x = self.g.pos
        self.e1.wait()
        p = self.g.p1
        total = self.u[p].astype(F32)
        for k in range(1, 4):
            total += self.r2[rem4(p + k)].astype(F32)
        self.v[...] = total.astype(BF16)
        for t in range(3):

            @pl.when(zl != t)
            def _():
                ref = self.v.at[pl.ds(16 * t, 16)]
                self.one(1 + t, ref, self.ra.at[zl], at(dp, y, t, core, x), 1 + zl).start()

    def step4(self):
        dp, y, zl, core, x = self.g.pos

        @pl.when(zl < 3)
        def _():
            total = self.v[pl.ds(pl.multiple_of(16 * zl, 16), 16)].astype(F32)
            for k in range(1, 4):
                source = rem4(zl + k)
                self.one(1, self.ra.at[source], self.ra.at[source], self.twin_id(), 1 + source).wait_recv()
                total += self.ra[source].astype(F32)
            self.va[...] = total.astype(BF16)

            @pl.when(dp != y)
            def _():
                self.one(4, self.va, self.rb.at[dp], at(y, y, zl, core, x), 5 + dp).start()

    def others(self):
        dp, y, zl, core, x = self.g.pos
        for k in range(1, 16):
            chip = lax.rem(y * 4 + zl + k, 16)
            yield k, (dp, chip * 2 + core, x)

    def step5(self):
        dp, y, zl, core, x = self.g.pos

        @pl.when((zl < 3) & (dp == y))
        def _():
            total = self.va[...].astype(F32)
            for k in range(1, 4):
                source = rem4(dp + k)
                self.one(1, self.va, self.rb.at[source], self.twin_id(), 5 + source).wait_recv()
                total += self.rb[source].astype(F32)
            ref = self.f.at[core, pl.ds(pl.multiple_of(16 * zl, 16), 16)]
            ref[...] = total.astype(BF16)
            for k, target in self.others():
                self.one(15 + k, ref, ref, target, 9 + zl).start()

    def step6(self):
        dp, y, zl, core, x = self.g.pos
        whole = self.f.at[core]
        for t in range(3):

            @pl.when((dp != y) | (zl != t))
            def _():
                ref = self.f.at[core, pl.ds(16 * t, 16)]
                self.one(1, ref, ref, self.twin_id(), 9 + t).wait_recv()

        self.one(11, whole, whole, self.twin_id(), 13).start()

    def step7(self, out):
        dp, y, zl, core, x = self.g.pos
        other = self.f.at[1 - core]
        self.one(11, other, other, self.twin_id(), 13).wait_recv()
        out[:, :640] = self.f[0][:36].astype(F32)
        out[:, 640:] = self.f[1][:36, :512].astype(F32)

    def drain(self, att2, up2):
        dp, y, zl, core, x = self.g.pos
        third, whole = self.va, self.f.at[core]
        self.one(0, up2, up2, self.twin_id()).wait_send()
        self.one(12, att2, att2, self.twin_id()).wait_send()
        self.e2.drain()
        self.e1.drain()
        for t in range(3):

            @pl.when(zl != t)
            def _():
                self.one(1 + t, third, third, self.twin_id()).wait_send()

        @pl.when((zl < 3) & (dp != y))
        def _():
            self.one(4, third, third, self.twin_id()).wait_send()

        @pl.when((zl < 3) & (dp == y))
        def _():
            for k in range(1, 16):
                self.one(15 + k, third, third, self.twin_id()).wait_send()

        self.one(11, whole, whole, self.twin_id()).wait_send()


def halo_copies(low, high, from_low, from_high, sems, slot):
    dp, y, zl, core, x = coords()
    send, recv = sems
    return [
        pltpu.make_async_remote_copy(
            src_ref=src,
            dst_ref=dst,
            send_sem=send.at[slot, i],
            recv_sem=recv.at[slot, i],
            device_id=at(dp, y, zl, core, rem4(x + step)),
            device_id_type=MESH,
        )
        for i, (src, dst, step) in enumerate(((low, from_high, -1), (high, from_low, 1)))
    ]


def kernel(
    latents,
    upstream,
    modulation,
    space_qkv,
    space_out,
    time_qkv,
    time_out,
    pattern,
    time_mask,
    result,
    start_grad,
    out_grad,
    s,
):
    dp, y, zl, core, x = coords()
    gather = Gather((s["g0"], s["g1"], s["g2"]), s["g_send"], s["g_recv"])
    sems = (s["m_send"], s["m_recv"])
    halo_sems = (s["h_send"], s["h_recv"])

    def move(out, name, slot):
        return Move(out, s[name + "_out"], s[name + "_in"], sems, slot)

    lat_move = move(True, "lat", 0)
    up_move = move(True, "up", 1)
    att_move = move(True, "att", 2)
    back_att = move(False, "batt", 3)
    back_grad = move(False, "bgrad", 4)
    back_mid = move(False, "bmid", 5)

    def split(name, value):
        s[name + "_out"][...] = value.reshape(32, 4, value.shape[-1])

    def joined(name):
        return s[name + "_in"][...].reshape(ROWS, -1)
    total = Total(
        gather,
        [s[n] for n in ("term", "r1", "u", "r2", "v", "ra", "va", "rb", "f")],
        (s["t_send"], s["t_recv"]),
        (s["o_send"], s["o_recv"]),
    )

    place_own(gather, space_qkv, space_out, time_qkv, time_out)
    greet()
    for g in range(3):
        gather.zsend(g)
    low, high = pl.ds(0, 64), pl.ds(64, 64)
    edge = s["edge"]
    halo = halo_copies(latents.at[low], latents.at[high], edge.at[low], edge.at[high], halo_sems, 0)
    for copy in halo:
        copy.start()

    start = latents[...].astype(F32)
    gain_space = 1.0 + modulation[0:1, :]
    gain_time = 1.0 + modulation[1:2, :]
    inverse = inverse_of(start)
    s["inv_s"][...] = inverse
    s["normed"][:ROWS] = (start * inverse * gain_space).astype(BF16)
    split("lat", latents[...])
    split("up", upstream[...])

    gather.zpass(0)
    gather.open(0)
    gather.zpass(1)
    gather.zpass(2)
    gather.s1mid(0)
    gather.open(1)
    gather.mid(0, 0)
    gather.s1end(0)
    gather.open(2)
    lat_move.start()
    gather.mid(0, 1, 3)
    gather.s1mid(1)
    gather.mid(0, 2)
    up_move.start()
    gather.s1end(1)
    gather.mid(1, 0)
    for copy in halo:
        copy.wait_recv()
    start = edge[...].astype(F32)
    s["normed"][ROWS:] = (start * inverse_of(start) * gain_space).astype(BF16)
    s["sbias"][...] = space_bias(pattern, x)
    s["tbias"][...] = time_bias(time_mask)
    gather.s1mid(2)
    gather.fin(0, 0, 1, 3)
    gather.mid(1, 1, 3)
    gather.s1end(2)
    gather.fin(0, 2)
    gather.mid(2, 0)
    join_qkv(s["g0"], s["w0"], core)
    gather.end(0)
    join_qkv(s["g0"], s["w0"], 1 - core)
    gather.mid(1, 2)
    kv = s["kv"]
    s["q"][...] = dot(s["normed"][:ROWS], s["w0"][:, :WIDE]).astype(BF16)
    rows = dot(s["normed"][...], s["w0"][:, 512:])
    kv[0] = rows[:, 64 : 64 + WIDE].astype(BF16)
    kv[1] = rows[:, WIDE : 2 * WIDE].astype(BF16)
    gather.mid(2, 1, 3)
    attend(s["q"], kv.at[0], kv.at[1], s["sbias"][...], s["probs_s"], s["acc"])
    att = s["acc"][...].astype(BF16)
    split("att", att)
    att_move.start()
    gather.mid(2, 2)
    gather.fin(1, 0, 1, 3, 2)
    join_out(s["g1"], s["so"], s["to"], core)
    gather.end(1)
    join_out(s["g1"], s["so"], s["to"], 1 - core)
    gather.fin(2, 0, 1, 3)
    s["mid_f"][...] = latents[...].astype(F32) + dot(att[:, :WIDTH], s["so"][:, :D])
    gather.fin(2, 2)
    up_move.finish()
    total.share(s["up_in"], s["up2"])
    s["up"][...] = joined("up")
    s["tgrad"][:, :WIDTH] = dot_nt(s["up"][...], s["to"][:, :D]).astype(BF16)
    s["tgrad"][:, WIDTH:] = jnp.zeros((ROWS, WIDE - WIDTH), BF16)
    lat_move.finish()
    att_move.finish()

    middle = joined("lat").astype(F32) + dot(joined("att")[:, :WIDTH], s["so"][:, :D])
    inverse = inverse_of(middle)
    s["inv_t"][...] = inverse
    s["mid_p"][...] = middle
    join_qkv(s["g2"], s["w2"], core)
    gather.end(2)
    join_qkv(s["g2"], s["w2"], 1 - core)
    rows = dot((middle * inverse * gain_time).astype(BF16), s["w2"][...])
    s["tq"][...] = rows[:, :WIDE].astype(BF16)
    s["tk"][...] = rows[:, WIDTH : WIDTH + WIDE].astype(BF16)
    s["tv"][...] = rows[:, 2 * WIDTH : 2 * WIDTH + WIDE].astype(BF16)
    attend(s["tq"], s["tk"], s["tv"], s["tbias"][...], s["probs_t"], s["acc"])
    s["tatt"][...] = s["acc"][...].astype(BF16)
    total.give(s["tatt"], s["tatt2"])
    split("batt", s["tatt"][...])

    attend_back(s["tq"], s["tk"], s["tv"], s["probs_t"], s["tgrad"], s["acc"], s["tdk"], s["tdv"])
    s["grads"][:, :WIDTH] = s["acc"][:, :WIDTH].astype(BF16)
    s["grads"][:, WIDTH : 2 * WIDTH] = s["tdk"][:, :WIDTH].astype(BF16)
    s["grads"][:, 2 * WIDTH :] = s["tdv"][...].astype(BF16)
    total.step1(s["tatt"], s["tatt2"], s["up"], s["up_in"], s["up2"])
    grad = dot_nt(s["grads"][...], s["w2"][...])
    mid_grad = s["up"][...].astype(F32) + norm_back(s["mid_p"][...], s["inv_t"][...], gain_time, grad)
    s["mid_grad"][...] = mid_grad.astype(BF16)
    s["sgrad"][:, :WIDTH] = dot_nt(s["mid_grad"][...], s["so"][:, :D]).astype(BF16)
    s["sgrad"][:, WIDTH:] = jnp.zeros((ROWS, WIDE - WIDTH), BF16)
    split("bgrad", s["sgrad"][...])
    back_grad.start()
    back_att.start()
    split("bmid", s["mid_grad"][...])
    back_mid.start()
    total.step2()
    total.step3()
    back_grad.finish()
    s["sgrad"][...] = joined("bgrad")

    space_back_rim(s["q"], kv.at[1], s["probs_s"], s["sgrad"], s["ds"], s["rim32"])
    s["rim"][...] = s["rim32"][...].astype(BF16)
    out_rim, in_rim = s["rim"], s["rim_in"]
    rim = halo_copies(
        out_rim.at[:, low], out_rim.at[:, high], in_rim.at[:, low], in_rim.at[:, high], halo_sems, 1
    )
    for copy in rim:
        copy.start()
    total.step4()
    space_back_own(s["q"], kv.at[0], s["probs_s"], s["sgrad"], s["ds"], s["acc"], s["dkv"])
    grad = dot_nt(s["acc"][...].astype(BF16), s["w0"][:, :WIDE])
    total.step5()
    back_att.finish()
    result[...] = (s["mid_f"][...] + dot(joined("batt")[:, :WIDTH], s["to"][:, :D])).astype(BF16)
    for copy in rim:
        copy.wait_recv()
    own = (s["dkv"][...] + in_rim[...].astype(F32)).astype(BF16)
    s["grads"][:, WIDTH : 2 * WIDTH] = own[0][:, :WIDTH]
    s["grads"][:, 2 * WIDTH :] = own[1]
    s["grads"][:, 512:WIDTH] = jnp.zeros((ROWS, 64), BF16)
    grad += dot_nt(s["grads"][:, 512:], s["w0"][:, 512:])
    back_mid.finish()
    start = latents[...].astype(F32)
    back = norm_back(start, s["inv_s"][...], gain_space, grad)
    start_grad[...] = (joined("bmid").astype(F32) + back).astype(BF16)
    total.step6()
    total.step7(out_grad)

    for g in range(3):
        gather.drain(g)
    for each in (lat_move, up_move, att_move, back_att, back_grad, back_mid):
        each.drain()
    total.drain(s["tatt2"], s["up2"])
    for copy in halo + rim:
        copy.wait_send()


def scratch():
    def vmem(shape, dtype=BF16):
        return pltpu.VMEM(shape, dtype)

    dma = pltpu.SemaphoreType.DMA
    out = {f"g{g}": vmem((2, 4, 4, 9, 8, lanes)) for g, lanes in enumerate(LANES)}
    out.update(g_send=dma((3, 56)), g_recv=dma((3, 56)), m_send=dma((6, 32)), m_recv=dma((6, 32)))
    out.update(h_send=dma((2, 2)), h_recv=dma((2, 2)), t_send=dma((2, 3)), t_recv=dma((2, 3)))
    out.update(o_send=dma((32,)), o_recv=dma((16,)))
    out.update(w0=vmem((D, 1792)), w2=vmem((D, 1792)), so=vmem((WIDTH, 1280)), to=vmem((WIDTH, 1280)))
    for name, lanes in (("lat", D), ("up", D), ("att", WIDE), ("batt", WIDE), ("bgrad", WIDE), ("bmid", D)):
        out[name + "_out"], out[name + "_in"] = vmem((32, 4, lanes)), vmem((32, 4, lanes))
    for name in ("tatt", "tatt2", "q", "tq", "tk", "tv", "tgrad", "sgrad"):
        out[name] = vmem((ROWS, WIDE))
    out.update(normed=vmem((256, D)), mid_grad=vmem((ROWS, D)), up=vmem((ROWS, D)), up2=vmem((32, 4, D)))
    out.update(kv=vmem((2, 256, WIDE)), grads=vmem((ROWS, 1792)))
    out.update(rim=vmem((2, ROWS, WIDE)), rim_in=vmem((2, ROWS, WIDE)), edge=vmem((ROWS, D)))
    out.update(inv_s=vmem((ROWS, 1), F32), inv_t=vmem((ROWS, 1), F32), tbias=vmem((ROWS, ROWS), F32), sbias=vmem((ROWS, 256), F32))
    out.update(acc=vmem((ROWS, WIDE), F32), tdk=vmem((ROWS, WIDE), F32), tdv=vmem((ROWS, WIDE), F32))
    out.update(dkv=vmem((2, ROWS, WIDE), F32), rim32=vmem((2, ROWS, WIDE), F32), ds=vmem((HEADS, ROWS, 256)), mid_f=vmem((ROWS, D), F32), mid_p=vmem((ROWS, D), F32))
    out.update(probs_s=vmem((HEADS, ROWS, 256), F32), probs_t=vmem((HEADS, ROWS, ROWS), F32))
    block = (48, WIDE)
    out.update(term=vmem((4, 4) + block), r1=vmem((4, 4) + block))
    out.update(u=vmem((4,) + block), r2=vmem((4,) + block), v=vmem(block), ra=vmem((4, 16, WIDE)))
    out.update(va=vmem((16, WIDE)), rb=vmem((4, 16, WIDE)), f=vmem((2,) + block))
    return out


def local(
    latents,
    upstream,
    modulation,
    space_qkv,
    space_out,
    time_qkv,
    time_out,
    space_pattern,
    time_mask,
):
    shapes = scratch()
    names = list(shapes)

    def body(*refs):
        kernel(*refs[:12], dict(zip(names, refs[12:])))

    vmem = pl.BlockSpec(memory_space=pltpu.VMEM)
    smem = pl.BlockSpec(memory_space=pltpu.SMEM)
    result, start_grad, out_grad = pl.pallas_call(
        body,
        out_shape=[
            jax.ShapeDtypeStruct((ROWS, D), BF16),
            jax.ShapeDtypeStruct((ROWS, D), BF16),
            jax.ShapeDtypeStruct((36, D), F32),
        ],
        in_specs=[vmem] * 7 + [smem, vmem],
        out_specs=[vmem] * 3,
        scratch_shapes=list(shapes.values()),
        compiler_params=pltpu.CompilerParams(
            collective_id=0, has_side_effects=True, vmem_limit_bytes=60 << 20
        ),
    )(
        latents.reshape(ROWS, D),
        upstream.reshape(ROWS, D),
        modulation.reshape(2, D),
        space_qkv,
        space_out,
        time_qkv,
        time_out,
        space_pattern,
        time_mask,
    )
    return (result.reshape(latents.shape), start_grad.reshape(latents.shape), out_grad)


def solution(mesh):
    in_specs = (
        P("dp", "seq", "tile", None),
        P("dp", "seq", "tile", None),
        P("dp", None, None),
        P(("dp", "tile"), None),
        P(("dp", "tile"), None),
        P(("dp", "tile"), None),
        P(("dp", "tile"), None),
        P("tile", None),
        P(),
    )
    out_specs = (
        P("dp", "seq", "tile", None),
        P("dp", "seq", "tile", None),
        P(("dp", "tile"), None),
    )
    return jax.shard_map(local, mesh=mesh, in_specs=in_specs, out_specs=out_specs, check_vma=False)
```

time: 139 us -> 126 us (0.906)
  the two profiles are of different devices: /device:TPU:19 before, /device:TPU:1 now
where the time goes in v3:
time: 126 us
  Pallas kernels  122 us (97%)
  local copies, waits for them, and re-layouts  3.45 us (3%)
    pallas_call x1, Pallas kernels, local(): pl.pallas_call(body, out_shape=[jax.ShapeDtypeStruct((ROWS, D), BF16), ja...  122 us
    unnamed x7, local copies, waits for them, and re-layouts  3.45 us

profile of v3, /device:TPU:1, one launch (start us, length us, event | category | flops | bytes accessed | tf_op | source)
XLA Modules:
  0.0 125.8 jit_solution(15036031989837716855)
XLA Ops:
  0.6 121.7 %shard_map.112 = (bf16[128,1152]{1,0:T(8,128)(2,1)}, bf16[128,1152]{1,0:T(8,128)(2,1)}, f32[36,1152]{1,0:T(8,128)}) custom-call(bf16[128,1152]{1,0:T(8,128)(2,1)} %bitcast.5, bf16[128,1152]{1,0:T(8,128)(2,1)} %bitcast.6, f32[2,1152]{1,0:T(2,128)} %bitcast.9, bf16[72,1728]{1,0:T(8,128)(2,1)} %refs_3_.1, bf16[36,1152]{1,0:T(8,128)(2,1)} %refs_4_.1, ...), custom_call_target="tpu_custom_call" | custom-call | tf_op jit(solution)/shard_map/pallas_call | solution.py:906
  122.3 0.0 copy-start
  122.3 1.7 %copy.15 = bf16[1,1,128,1152]{3,2,1,0:T(8,128)(2,1)} copy(bf16[1,1,128,1152]{3,2,1,0:T(8,128)(2,1)} %bitcast.8) | data formatting | bytes 589824
  124.1 0.0 copy-done
  124.1 0.0 copy-start.1
  124.1 0.7 copy.16
  124.8 0.3 copy-done.1
  125.1 0.7 copy.17
Async XLA Ops:
  122.3 1.8 %copy-start = (bf16[128,1152]{1,0:T(8,128)(2,1)S(1)}, bf16[128,1152]{1,0:T(8,128)(2,1)}, u32[]{:S(2)}) copy-start(bf16[128,1152]{1,0:T(8,128)(2,1)} %get-tuple-element.7) | copy-start | bytes 884740
  124.1 1.0 copy-start.1

commit v4 on v3

--- a/solution.py
+++ b/solution.py
@@ -524,21 +524,23 @@
 
     def step1(self, att, att2, up, up_in, up2):
         dp, y, zl, core, x = self.g.pos
-        self.one(0, up_in, up2, self.twin_id()).wait_recv()
-        self.one(12, att, att2, self.twin_id(), 14).wait_recv()
         for half in range(2):
 
             @pl.when(core == half)
             def _():
                 lanes = slice(0, 640) if half == 0 else slice(640, D)
                 term = dot_tn(att[:, :WIDTH], up[:, lanes])
+                self.one(0, up_in, up2, self.twin_id()).wait_recv()
+                self.one(12, att, att2, self.twin_id(), 14).wait_recv()
                 term += dot_tn(att2[:, :WIDTH], up2[:, :, lanes].reshape(ROWS, -1))
                 if half == 1:
                     term = jnp.concatenate([term, jnp.zeros((WIDTH, 128), F32)], axis=1)
-                for i in range(16):
-                    block = jnp.concatenate([term[36 * i : 36 * i + 36], jnp.zeros((12, 640), F32)], axis=0)
-                    place = (i % 4, i // 4) if half == 0 else (i // 4, i % 4)
-                    self.term[place] = block.astype(BF16)
+                for i in range(4):
+                    if half == 0:
+                        rows = [term[36 * (4 * j + i) : 36 * (4 * j + i) + 36] for j in range(4)]
+                        self.term[i] = jnp.concatenate(rows, axis=0).astype(BF16)
+                    else:
+                        self.term[i] = term[144 * i : 144 * i + 144].astype(BF16)
 
         self.e2.start()
 
@@ -549,7 +551,9 @@
         total = self.term[p].astype(F32)
         for k in range(1, 4):
             total += self.r1[rem4(p + k)].astype(F32)
-        self.u[...] = total.astype(BF16)
+        for i in range(4):
+            block = jnp.concatenate([total[36 * i : 36 * i + 36], jnp.zeros((12, 640), F32)], axis=0)
+            self.u[i] = block.astype(BF16)
         self.e1.start()
 
     def step3(self):
@@ -797,13 +801,11 @@
     attend(s["tq"], s["tk"], s["tv"], s["tbias"][...], s["probs_t"], s["acc"])
     s["tatt"][...] = s["acc"][...].astype(BF16)
     total.give(s["tatt"], s["tatt2"])
-    split("batt", s["tatt"][...])
-
+    total.step1(s["tatt"], s["tatt2"], s["up"], s["up_in"], s["up2"])
     attend_back(s["tq"], s["tk"], s["tv"], s["probs_t"], s["tgrad"], s["acc"], s["tdk"], s["tdv"])
     s["grads"][:, :WIDTH] = s["acc"][:, :WIDTH].astype(BF16)
     s["grads"][:, WIDTH : 2 * WIDTH] = s["tdk"][:, :WIDTH].astype(BF16)
     s["grads"][:, 2 * WIDTH :] = s["tdv"][...].astype(BF16)
-    total.step1(s["tatt"], s["tatt2"], s["up"], s["up_in"], s["up2"])
     grad = dot_nt(s["grads"][...], s["w2"][...])
     mid_grad = s["up"][...].astype(F32) + norm_back(s["mid_p"][...], s["inv_t"][...], gain_time, grad)
     s["mid_grad"][...] = mid_grad.astype(BF16)
@@ -811,11 +813,17 @@
     s["sgrad"][:, WIDTH:] = jnp.zeros((ROWS, WIDE - WIDTH), BF16)
     split("bgrad", s["sgrad"][...])
     back_grad.start()
+    split("batt", s["tatt"][...])
+    split("bmid", s["mid_grad"][...])
+    total.step2()
     back_att.start()
-    split("bmid", s["mid_grad"][...])
+    gather.drain(0)
+    gather.drain(1)
+    total.step3()
     back_mid.start()
-    total.step2()
-    total.step3()
+    gather.drain(2)
+    for each in (lat_move, up_move, att_move):
+        each.drain()
     back_grad.finish()
     s["sgrad"][...] = joined("bgrad")
 
@@ -841,19 +849,16 @@
     s["grads"][:, 512:WIDTH] = jnp.zeros((ROWS, 64), BF16)
     grad += dot_nt(s["grads"][:, 512:], s["w0"][:, 512:])
     back_mid.finish()
+    total.step6()
     start = latents[...].astype(F32)
     back = norm_back(start, s["inv_s"][...], gain_space, grad)
     start_grad[...] = (joined("bmid").astype(F32) + back).astype(BF16)
-    total.step6()
-    total.step7(out_grad)
-
-    for g in range(3):
-        gather.drain(g)
-    for each in (lat_move, up_move, att_move, back_att, back_grad, back_mid):
+    for each in (back_att, back_grad, back_mid):
         each.drain()
-    total.drain(s["tatt2"], s["up2"])
     for copy in halo + rim:
         copy.wait_send()
+    total.step7(out_grad)
+    total.drain(s["tatt2"], s["up2"])
 
 
 def scratch():
@@ -878,7 +883,7 @@
     out.update(dkv=vmem((2, ROWS, WIDE), F32), rim32=vmem((2, ROWS, WIDE), F32), ds=vmem((HEADS, ROWS, 256)), mid_f=vmem((ROWS, D), F32), mid_p=vmem((ROWS, D), F32))
     out.update(probs_s=vmem((HEADS, ROWS, 256), F32), probs_t=vmem((HEADS, ROWS, ROWS), F32))
     block = (48, WIDE)
-    out.update(term=vmem((4, 4) + block), r1=vmem((4, 4) + block))
+    out.update(term=vmem((4, 144, WIDE)), r1=vmem((4, 144, WIDE)))
     out.update(u=vmem((4,) + block), r2=vmem((4,) + block), v=vmem(block), ra=vmem((4, 16, WIDE)))
     out.update(va=vmem((16, WIDE)), rb=vmem((4, 16, WIDE)), f=vmem((2,) + block))
     return out

time: 126 us -> 120 us (0.952)
  Pallas kernels: 122 us -> 116 us
    pallas_call x1, Pallas kernels: 122 us -> 116 us  [local(): pl.pallas_call(body, out_shape=[jax.ShapeDtypeStruct((ROWS, D), BF16), ja...]
where the time goes in v4:
time: 120 us
  Pallas kernels  116 us (97%)
  local copies, waits for them, and re-layouts  3.45 us (3%)
    pallas_call x1, Pallas kernels, local(): pl.pallas_call(body, out_shape=[jax.ShapeDtypeStruct((ROWS, D), BF16), ja...  116 us
    unnamed x7, local copies, waits for them, and re-layouts  3.45 us

profile of v4, /device:TPU:1, one launch (start us, length us, event | category | flops | bytes accessed | tf_op | source)
XLA Modules:
  0.0 120.1 jit_solution(3218067864305040652)
XLA Ops:
  0.6 116.0 %shard_map.112 = (bf16[128,1152]{1,0:T(8,128)(2,1)}, bf16[128,1152]{1,0:T(8,128)(2,1)}, f32[36,1152]{1,0:T(8,128)}) custom-call(bf16[128,1152]{1,0:T(8,128)(2,1)} %bitcast.5, bf16[128,1152]{1,0:T(8,128)(2,1)} %bitcast.6, f32[2,1152]{1,0:T(2,128)} %bitcast.9, bf16[72,1728]{1,0:T(8,128)(2,1)} %refs_3_.1, bf16[36,1152]{1,0:T(8,128)(2,1)} %refs_4_.1, ...), custom_call_target="tpu_custom_call" | custom-call | tf_op jit(solution)/shard_map/pallas_call | solution.py:911
  116.6 0.0 copy-start
  116.6 1.7 %copy.15 = bf16[1,1,128,1152]{3,2,1,0:T(8,128)(2,1)} copy(bf16[1,1,128,1152]{3,2,1,0:T(8,128)(2,1)} %bitcast.8) | data formatting | bytes 589824
  118.4 0.0 copy-done
  118.4 0.0 copy-start.1
  118.4 0.7 copy.16
  119.1 0.3 copy-done.1
  119.4 0.7 copy.17
Async XLA Ops:
  116.6 1.8 %copy-start = (bf16[128,1152]{1,0:T(8,128)(2,1)S(1)}, bf16[128,1152]{1,0:T(8,128)(2,1)}, u32[]{:S(2)}) copy-start(bf16[128,1152]{1,0:T(8,128)(2,1)} %get-tuple-element.7) | copy-start | bytes 884740
  118.4 1.0 copy-start.1

commit v5 on v4

--- a/solution.py
+++ b/solution.py
@@ -230,7 +230,6 @@
         hello(at(dp, y, zl, core, rem4(x + k)))
     for step in (1, 3):
         hello(at(rem4(dp + step), y, 3 - zl, core, x))
-    pl.semaphore_wait(barrier, 39)
 
 
 def place_own(gather, space_qkv, space_out, time_qkv, time_out):
@@ -278,7 +277,7 @@
         )
 
     def start(self):
-        for k in range(1, self.n):
+        for k in (2, 1, 3):
             other = lax.rem(self.me + k, self.n)
             self.copy(k, self.block(other), self.slot(self.me), self.target(other)).start()
 
@@ -710,8 +709,9 @@
         (s["o_send"], s["o_recv"]),
     )
 
+    greet()
     place_own(gather, space_qkv, space_out, time_qkv, time_out)
-    greet()
+    pl.semaphore_wait(pltpu.get_barrier_semaphore(), 39)
     for g in range(3):
         gather.zsend(g)
     low, high = pl.ds(0, 64), pl.ds(64, 64)
@@ -735,14 +735,14 @@
     gather.zpass(2)
     gather.s1mid(0)
     gather.open(1)
+    up_move.start()
+    lat_move.start()
     gather.mid(0, 0)
     gather.s1end(0)
     gather.open(2)
-    lat_move.start()
     gather.mid(0, 1, 3)
     gather.s1mid(1)
     gather.mid(0, 2)
-    up_move.start()
     gather.s1end(1)
     gather.mid(1, 0)
     for copy in halo:
@@ -779,6 +779,7 @@
     gather.fin(2, 0, 1, 3)
     s["mid_f"][...] = latents[...].astype(F32) + dot(att[:, :WIDTH], s["so"][:, :D])
     gather.fin(2, 2)
+    join_qkv(s["g2"], s["w2"], core)
     up_move.finish()
     total.share(s["up_in"], s["up2"])
     s["up"][...] = joined("up")
@@ -791,7 +792,6 @@
     inverse = inverse_of(middle)
     s["inv_t"][...] = inverse
     s["mid_p"][...] = middle
-    join_qkv(s["g2"], s["w2"], core)
     gather.end(2)
     join_qkv(s["g2"], s["w2"], 1 - core)
     rows = dot((middle * inverse * gain_time).astype(BF16), s["w2"][...])

time: 120 us -> 120 us (level)
  no operation moved by 1% of the time
where the time goes in v5:
time: 120 us
  Pallas kernels  116 us (97%)
  local copies, waits for them, and re-layouts  3.45 us (3%)
    pallas_call x1, Pallas kernels, local(): pl.pallas_call(body, out_shape=[jax.ShapeDtypeStruct((ROWS, D), BF16), ja...  116 us
    unnamed x7, local copies, waits for them, and re-layouts  3.45 us

profile of v5, /device:TPU:1, one launch (start us, length us, event | category | flops | bytes accessed | tf_op | source)
XLA Modules:
  0.0 119.8 jit_solution(4166174396589832840)
XLA Ops:
  0.6 115.7 %shard_map.112 = (bf16[128,1152]{1,0:T(8,128)(2,1)}, bf16[128,1152]{1,0:T(8,128)(2,1)}, f32[36,1152]{1,0:T(8,128)}) custom-call(bf16[128,1152]{1,0:T(8,128)(2,1)} %bitcast.5, bf16[128,1152]{1,0:T(8,128)(2,1)} %bitcast.6, f32[2,1152]{1,0:T(2,128)} %bitcast.9, bf16[72,1728]{1,0:T(8,128)(2,1)} %refs_3_.1, bf16[36,1152]{1,0:T(8,128)(2,1)} %refs_4_.1, ...), custom_call_target="tpu_custom_call" | custom-call | tf_op jit(solution)/shard_map/pallas_call | solution.py:911
  116.4 0.0 copy-start
  116.4 1.7 %copy.15 = bf16[1,1,128,1152]{3,2,1,0:T(8,128)(2,1)} copy(bf16[1,1,128,1152]{3,2,1,0:T(8,128)(2,1)} %bitcast.8) | data formatting | bytes 589824
  118.1 0.0 copy-done
  118.1 0.0 copy-start.1
  118.1 0.7 copy.16
  118.8 0.3 copy-done.1
  119.1 0.7 copy.17
Async XLA Ops:
  116.4 1.8 %copy-start = (bf16[128,1152]{1,0:T(8,128)(2,1)S(1)}, bf16[128,1152]{1,0:T(8,128)(2,1)}, u32[]{:S(2)}) copy-start(bf16[128,1152]{1,0:T(8,128)(2,1)} %get-tuple-element.7) | copy-start | bytes 884740
  118.1 1.0 copy-start.1
